TPU v7x, 512 devices: a whole 4x8x8 slice. The times are simulated.
512 devices in a mesh: wide: 64 (over y, x, core), narrow: 8 (over z).
Axes of the slice: x: 4, y: 8, z: 8, core: 2. Of those that a mesh axis runs over, the one named last changes fastest.
Arguments:
- right_side: float32 [512, 128, 256], P('wide', 'narrow'), may hold values from -8 to 8
- coefficient: float32 [512, 128, 256], P('wide', 'narrow'), may hold values from 0.2 to 5
Outputs:
- correction: float32 [512, 128, 256], P('wide', 'narrow')
All inputs are finite; a program needn't handle non-finite values.
Results may differ from a plain program's by a relative error of at most 0.0001.
Values sent between devices are 32-bit elements; how exact they have to be, the bound alone decides.
A program may use at most 64 MiB of HBM per device.

v0:
```python
import jax
import jax.numpy as jnp
from jax import lax
from jax.sharding import PartitionSpec as P

COARSE_ITERS = 5


OMEGA = 0.8


def with_halo(array, sides, width):
    for axis, dim in sides:
        size, length = (lax.axis_size(axis), array.shape[dim])
        up = [(i, (i + 1) % size) for i in range(size - 1)]
        down = [(j, i) for i, j in up]
        last = lax.slice_in_dim(array, length - width, length, axis=dim)
        leading = lax.slice_in_dim(array, 0, width, axis=dim)
        before = lax.ppermute(last, axis, up)
        after = lax.ppermute(leading, axis, down)
        array = jnp.concatenate([before, array, after], axis=dim)
    return array


def pad_plane(x):
    return jnp.pad(x, ((1, 1), (1, 1), (0, 0)))


def neighbours(vx, kx):
    vz = jnp.pad(vx[1:-1, 1:-1], ((0, 0), (0, 0), (1, 1)))
    kz = jnp.pad(kx[1:-1, 1:-1], ((0, 0), (0, 0), (1, 1)))
    return [
        (vx[2:, 1:-1], kx[2:, 1:-1]),
        (vx[:-2, 1:-1], kx[:-2, 1:-1]),
        (vx[1:-1, 2:], kx[1:-1, 2:]),
        (vx[1:-1, :-2], kx[1:-1, :-2]),
        (vz[:, :, 2:], kz[:, :, 2:]),
        (vz[:, :, :-2], kz[:, :, :-2]),
    ]


def local_apply(vx, kx):
    center = vx[1:-1, 1:-1]
    kc = kx[1:-1, 1:-1]
    image = jnp.zeros_like(center)
    diag = jnp.zeros_like(center)
    for vn, kn in neighbours(vx, kx):
        face = 0.5 * (kc + kn)
        image = image + face * (center - vn)
        diag = diag + face
    return (image, diag)


def diag_only(kx):
    kc = kx[1:-1, 1:-1]
    kz = jnp.pad(kc, ((0, 0), (0, 0), (1, 1)))
    diag = jnp.zeros_like(kc)
    for kn in [
        kx[2:, 1:-1],
        kx[:-2, 1:-1],
        kx[1:-1, 2:],
        kx[1:-1, :-2],
        kz[:, :, 2:],
        kz[:, :, :-2],
    ]:
        diag = diag + 0.5 * (kc + kn)
    return diag


def relax(ex, r, kx):
    image, diag = local_apply(ex, kx)
    return ex[1:-1, 1:-1] + OMEGA * (r - image) / diag


def restrict(x):
    a, b, c = x.shape
    return jnp.sum(x.reshape(a // 2, 2, b // 2, 2, c // 2, 2), axis=(1, 3, 5)) * 0.5


def coarsen(k):
    a, b, c = k.shape
    return jnp.sum(k.reshape(a // 2, 2, b // 2, 2, c // 2, 2), axis=(1, 3, 5)) * 0.125


def prolong(x):
    return jnp.repeat(jnp.repeat(jnp.repeat(x, 2, axis=0), 2, axis=1), 2, axis=2)


def descend(r, kx, extend):
    e = OMEGA * r / diag_only(kx)
    e = relax(extend(e), r, kx)
    image = local_apply(extend(e), kx)[0]
    return (e, restrict(r - image))


def ascend(e, r, kx, extend):
    e = relax(extend(e), r, kx)
    e = relax(extend(e), r, kx)
    return e


def coarse_solve(r, k):
    kx = pad_plane(k)
    solution = jnp.zeros_like(r)
    residual = r
    direction = r
    norm_now = jnp.sum(residual * residual)
    for step in range(COARSE_ITERS):
        image = local_apply(pad_plane(direction), kx)[0]
        alpha = norm_now / jnp.sum(direction * image)
        solution = solution + alpha * direction
        residual = residual - alpha * image
        norm_next = jnp.sum(residual * residual)
        direction = residual + norm_next / norm_now * direction
        norm_now = norm_next
    return solution


def brick_extend(x):
    return with_halo(x, (("wide", 0), ("narrow", 1)), 1)


def coef_extend(k):
    return with_halo(k, (("wide", 0), ("narrow", 1)), 2)


def plane_extend(x):
    grown = with_halo(x, (("wide", 0),), 1)
    return jnp.pad(grown, ((0, 0), (1, 1), (0, 0)))


def post_smooth(e, r, wide_kx):
    inner_kx = wide_kx[1:-1, 1:-1]
    return ascend(e, r, inner_kx, brick_extend)


def per_device(right_side, coefficient):
    wide_at = lax.axis_index("wide")
    narrow_at = lax.axis_index("narrow")
    k0_wide = coef_extend(coefficient)
    e0, r1 = descend(right_side, k0_wide[1:-1, 1:-1], brick_extend)
    k1 = coarsen(coefficient)
    k1_wide = coef_extend(k1)
    e1, r2 = descend(r1, k1_wide[1:-1, 1:-1], brick_extend)
    k2 = coarsen(k1)
    group_r, group_k = (
        lax.all_gather(r2, "narrow", axis=1, tiled=True),
        lax.all_gather(k2, "narrow", axis=1, tiled=True),
    )
    k2x = plane_extend(group_k)
    e2, r3 = descend(group_r, k2x, plane_extend)
    k3 = coarsen(group_k)
    whole_r, whole_k = (
        lax.all_gather(r3, "wide", axis=0, tiled=True),
        lax.all_gather(k3, "wide", axis=0, tiled=True),
    )
    e3 = coarse_solve(whole_r, whole_k)
    mine = lax.dynamic_slice_in_dim(e3, wide_at * r3.shape[0], r3.shape[0], 0)
    e2 = ascend(e2 + prolong(mine), group_r, k2x, plane_extend)
    e2 = lax.dynamic_slice_in_dim(e2, narrow_at * r2.shape[1], r2.shape[1], 1)
    e1 = post_smooth(e1 + prolong(e2), r1, k1_wide)
    e0 = post_smooth(e0 + prolong(e1), right_side, k0_wide)
    return e0


def solution(mesh):
    placed = (P("wide", "narrow", None), P("wide", "narrow", None))
    return jax.shard_map(
        per_device, mesh=mesh, in_specs=placed, out_specs=P("wide", "narrow", None), check_vma=False
    )
```

profile of v0, /device:TPU:224, one launch (start us, length us, event | category | flops | bytes accessed | tf_op | source)
XLA Modules:
  0.0 468.1 jit_solution(3177788665440263589)
XLA Ops:
  2.7 7.0 %collective-permute-start = (f32[2,16,256]{2,1,0:T(8,128)S(1)}, f32[2,16,256]{2,1,0:T(8,128)S(1)}, u32[]{:S(2)}, u32[]{:S(2)}) collective-permute-start(f32[2,16,256]{2,1,0:T(8,128)S(1)} %get-tuple-element.57), channel_id=1, source_target_pairs={{8,0},{16,8},{24,16},{32,24},{40,32},{48,40},{56,48},{64,56},{72,6... | collective-permute-start | bytes 98312 | tf_op jit(solution)/shard_map/ppermute | solution.py:20
  13.2 5.5 %collective-permute-start.3 = (f32[12,2,256]{2,1,0:T(2,128)S(1)}, f32[12,2,256]{2,1,0:T(2,128)S(1)}, u32[]{:S(2)}, u32[]{:S(2)}) collective-permute-start(f32[12,2,256]{2,1,0:T(2,128)S(1)} %get-tuple-element.38), channel_id=1, source_target_pairs={{0,1},{1,2},{2,3},{3,4},{4,5},{5,6},{6,7},{8,9},{9,10},{10,11},{11... | collective-permute-start | bytes 73736 | tf_op jit(solution)/shard_map/ppermute | solution.py:19
  21.6 6.1 %collective-permute-start.4 = (f32[1,16,256]{2,1,0:T(8,128)S(1)}, f32[1,16,256]{2,1,0:T(8,128)S(1)}, u32[]{:S(2)}, u32[]{:S(2)}) collective-permute-start(f32[1,16,256]{2,1,0:T(8,128)S(1)} %get-tuple-element.55), channel_id=1, source_target_pairs={{8,0},{16,8},{24,16},{32,24},{40,32},{48,40},{56,48},{64,56},{72,6... | collective-permute-start | bytes 49160 | tf_op jit(solution)/shard_map/ppermute | solution.py:20
  29.8 10.5 %reshape.64 = f32[4,2,8,2,128,2]{5,4,3,2,1,0:T(8,128)} reshape(f32[8,16,256]{2,1,0:T(8,128)} %param.3) | data formatting | bytes 262144 | tf_op jit(solution)/shard_map/reshape | solution.py:82
  40.3 4.0 reduce_sum.159
  46.3 5.1 %collective-permute-start.7 = (f32[10,1,256]{2,1,0:T(1,128)S(1)}, f32[10,1,256]{2,1,0:T(1,128)S(1)}, u32[]{:S(2)}, u32[]{:S(2)}) collective-permute-start(f32[10,1,256]{2,1,0:T(1,128)S(1)} %get-tuple-element.47), channel_id=1, source_target_pairs={{0,1},{1,2},{2,3},{3,4},{4,5},{5,6},{6,7},{8,9},{9,10},{10,11},{11... | collective-permute-start | bytes 30728 | tf_op jit(solution)/shard_map/ppermute | solution.py:19
  53.1 6.1 %collective-permute-start.8 = (f32[1,16,256]{2,1,0:T(8,128)S(1)}, f32[1,16,256]{2,1,0:T(8,128)S(1)}, u32[]{:S(2)}, u32[]{:S(2)}) collective-permute-start(f32[1,16,256]{2,1,0:T(8,128)S(1)} %get-tuple-element.53), channel_id=1, source_target_pairs={{8,0},{16,8},{24,16},{32,24},{40,32},{48,40},{56,48},{64,56},{72,6... | collective-permute-start | bytes 49160 | tf_op jit(solution)/shard_map/ppermute | solution.py:20
  61.1 7.0 %collective-permute-start.12 = (f32[2,8,128]{2,1,0:T(8,128)S(1)}, f32[2,8,128]{2,1,0:T(8,128)S(1)}, u32[]{:S(2)}, u32[]{:S(2)}) collective-permute-start(f32[2,8,128]{2,1,0:T(8,128)S(1)} %get-tuple-element.91), channel_id=1, source_target_pairs={{8,0},{16,8},{24,16},{32,24},{40,32},{48,40},{56,48},{64,56},{72,6... | collective-permute-start | bytes 24584 | tf_op jit(solution)/shard_map/ppermute | solution.py:20
  73.2 5.1 %collective-permute-start.11 = (f32[10,1,256]{2,1,0:T(1,128)S(1)}, f32[10,1,256]{2,1,0:T(1,128)S(1)}, u32[]{:S(2)}, u32[]{:S(2)}) collective-permute-start(f32[10,1,256]{2,1,0:T(1,128)S(1)} %get-tuple-element.45), channel_id=1, source_target_pairs={{0,1},{1,2},{2,3},{3,4},{4,5},{5,6},{6,7},{8,9},{9,10},{10,11},{11... | collective-permute-start | bytes 30728 | tf_op jit(solution)/shard_map/ppermute | solution.py:19
  80.3 5.1 %collective-permute-start.15 = (f32[8,2,128]{2,1,0:T(2,128)S(1)}, f32[8,2,128]{2,1,0:T(2,128)S(1)}, u32[]{:S(2)}, u32[]{:S(2)}) collective-permute-start(f32[8,2,128]{2,1,0:T(2,128)S(1)} %get-tuple-element.72), channel_id=1, source_target_pairs={{0,1},{1,2},{2,3},{3,4},{4,5},{5,6},{6,7},{8,9},{9,10},{10,11},{11... | collective-permute-start | bytes 24584 | tf_op jit(solution)/shard_map/ppermute | solution.py:19
  85.6 9.8 %reshape.63 = f32[4,2,8,2,128,2]{5,4,3,2,1,0:T(8,128)} reshape(f32[8,16,256]{2,1,0:T(8,128)S(1)} %fusion.93) | data formatting | bytes 262144 | tf_op jit(solution)/shard_map/reshape | solution.py:77
  99.6 6.1 %collective-permute-start.16 = (f32[1,8,128]{2,1,0:T(8,128)S(1)}, f32[1,8,128]{2,1,0:T(8,128)S(1)}, u32[]{:S(2)}, u32[]{:S(2)}) collective-permute-start(f32[1,8,128]{2,1,0:T(8,128)S(1)} %get-tuple-element.89), channel_id=1, source_target_pairs={{8,0},{16,8},{24,16},{32,24},{40,32},{48,40},{56,48},{64,56},{72,6... | collective-permute-start | bytes 12296 | tf_op jit(solution)/shard_map/ppermute | solution.py:20
  107.7 6.3 %collective-permute-done.17 = f32[1,8,128]{2,1,0:T(8,128)S(1)} collective-permute-done((f32[1,8,128]{2,1,0:T(8,128)S(1)}, f32[1,8,128]{2,1,0:T(8,128)S(1)}, u32[]{:S(2)}, u32[]{:S(2)}) %collective-permute-start.17) | collective-permute-done | bytes 4128 | tf_op jit(solution)/shard_map/ppermute | solution.py:19
  115.9 5.1 %collective-permute-start.19 = (f32[6,1,128]{2,1,0:T(1,128)S(1)}, f32[6,1,128]{2,1,0:T(1,128)S(1)}, u32[]{:S(2)}, u32[]{:S(2)}) collective-permute-start(f32[6,1,128]{2,1,0:T(1,128)S(1)} %get-tuple-element.81), channel_id=1, source_target_pairs={{0,1},{1,2},{2,3},{3,4},{4,5},{5,6},{6,7},{8,9},{9,10},{10,11},{11... | collective-permute-start | bytes 9224 | tf_op jit(solution)/shard_map/ppermute | solution.py:19
  121.1 24.5 %all_gather.13 = f32[2,32,64]{2,0,1:T(2,128)S(1)} all-gather(f32[2,4,64]{2,0,1:T(2,128)S(1)} %copy.329), channel_id=1, replica_groups=mesh['wide'=64,'narrow'=8] {'narrow'}, dimensions={1}, use_global_device_ids=true | all-gather | bytes 18432 | tf_op jit(solution)/shard_map/all_gather | solution.py:148
  150.0 6.5 %collective-permute-start.24 = (f32[1,32,64]{2,1,0:T(8,128)S(1)}, f32[1,32,64]{2,1,0:T(8,128)S(1)}, u32[]{:S(2)}, u32[]{:S(2)}) collective-permute-start(f32[1,32,64]{2,1,0:T(8,128)S(1)} %get-tuple-element.70), channel_id=1, source_target_pairs={{8,0},{16,8},{24,16},{32,24},{40,32},{48,40},{56,48},{64,56},{72,6... | collective-permute-start | bytes 24584 | tf_op jit(solution)/shard_map/ppermute | solution.py:20
  161.1 5.1 %collective-permute-start.23 = (f32[6,1,128]{2,1,0:T(1,128)S(1)}, f32[6,1,128]{2,1,0:T(1,128)S(1)}, u32[]{:S(2)}, u32[]{:S(2)}) collective-permute-start(f32[6,1,128]{2,1,0:T(1,128)S(1)} %get-tuple-element.79), channel_id=1, source_target_pairs={{0,1},{1,2},{2,3},{3,4},{4,5},{5,6},{6,7},{8,9},{9,10},{10,11},{11... | collective-permute-start | bytes 9224 | tf_op jit(solution)/shard_map/ppermute | solution.py:19
  168.9 24.7 %all_gather.12 = f32[2,32,64]{2,0,1:T(2,128)S(1)} all-gather(f32[2,4,64]{2,0,1:T(2,128)S(1)} %copy.327), channel_id=1, replica_groups=mesh['wide'=64,'narrow'=8] {'narrow'}, dimensions={1}, use_global_device_ids=true | all-gather | bytes 18432 | tf_op jit(solution)/shard_map/all_gather | solution.py:147
  198.6 5.9 %collective-permute-done.27 = f32[1,32,64]{2,1,0:T(8,128)S(1)} collective-permute-done((f32[1,32,64]{2,1,0:T(8,128)S(1)}, f32[1,32,64]{2,1,0:T(8,128)S(1)}, u32[]{:S(2)}, u32[]{:S(2)}) %collective-permute-start.27) | collective-permute-done | bytes 8224 | tf_op jit(solution)/shard_map/ppermute | solution.py:19
  209.1 53.8 %all-gather.1 = f32[1024,32]{1,0:T(8,128)} all-gather(f32[16,32]{1,0:T(8,128)S(1)} %broadcast_multiply_fusion.1), channel_id=3, replica_groups=mesh['wide'=64,'narrow'=8] {'wide'}, dimensions={0}, use_global_device_ids=true | all-gather | bytes 133120 | tf_op jit(solution)/shard_map/all_gather | solution.py:155
  263.8 48.0 %all-gather = f32[1024,32]{1,0:T(8,128)S(1)} all-gather(f32[16,32]{1,0:T(8,128)S(1)} %broadcast_multiply_fusion.2), channel_id=2, replica_groups=mesh['wide'=64,'narrow'=8] {'wide'}, dimensions={0}, use_global_device_ids=true | all-gather | bytes 133120 | tf_op jit(solution)/shard_map/all_gather | solution.py:154
  311.8 5.4 %multiply_reduce_fusion.7 = (f32[]{:T(128)}, f32[]{:T(128)}, f32[64,16,32]{2,1,0:T(8,128)}, f32[64,16,32]{2,1,0:T(8,128)S(1)}, f32[64,16,32]{2,1,0:T(8,128)S(1)}...) fusion(f32[64,16,32]{2,1,0:T(8,128)S(1)} %bitcast.16, ...), kind=kLoop, calls=%fused_computation.113 | loop fusion | flops 1081342 | bytes 1179656 | tf_op jit(solution)/shard_map/reduce_sum | solution.py:110
  359.3 4.6 collective-permute-start.30
  365.8 6.4 %collective-permute-done.31 = f32[1,32,64]{2,1,0:T(8,128)S(1)} collective-permute-done((f32[1,32,64]{2,1,0:T(8,128)S(1)}, f32[1,32,64]{2,1,0:T(8,128)S(1)}, u32[]{:S(2)}, u32[]{:S(2)}) %collective-permute-start.31) | collective-permute-done | bytes 8224 | tf_op jit(solution)/shard_map/ppermute | solution.py:19
  377.7 5.9 %collective-permute-done.33 = f32[1,32,64]{2,1,0:T(8,128)S(1)} collective-permute-done((f32[1,32,64]{2,1,0:T(8,128)S(1)}, f32[1,32,64]{2,1,0:T(8,128)S(1)}, u32[]{:S(2)}, u32[]{:S(2)}) %collective-permute-start.33) | collective-permute-done | bytes 8224 | tf_op jit(solution)/shard_map/ppermute | solution.py:19
  390.8 5.8 %collective-permute-done.35 = f32[1,8,128]{2,1,0:T(8,128)S(1)} collective-permute-done((f32[1,8,128]{2,1,0:T(8,128)S(1)}, f32[1,8,128]{2,1,0:T(8,128)S(1)}, u32[]{:S(2)}, u32[]{:S(2)}) %collective-permute-start.35) | collective-permute-done | bytes 4128 | tf_op jit(solution)/shard_map/ppermute | solution.py:19
  411.2 5.8 %collective-permute-done.39 = f32[1,8,128]{2,1,0:T(8,128)S(1)} collective-permute-done((f32[1,8,128]{2,1,0:T(8,128)S(1)}, f32[1,8,128]{2,1,0:T(8,128)S(1)}, u32[]{:S(2)}, u32[]{:S(2)}) %collective-permute-start.39) | collective-permute-done | bytes 4128 | tf_op jit(solution)/shard_map/ppermute | solution.py:19
  419.0 5.1 %collective-permute-start.41 = (f32[6,1,128]{2,1,0:T(1,128)S(1)}, f32[6,1,128]{2,1,0:T(1,128)S(1)}, u32[]{:S(2)}, u32[]{:S(2)}) collective-permute-start(f32[6,1,128]{2,1,0:T(1,128)S(1)} %get-tuple-element.75), channel_id=1, source_target_pairs={{0,1},{1,2},{2,3},{3,4},{4,5},{5,6},{6,7},{8,9},{9,10},{10,11},{11... | collective-permute-start | bytes 9224 | tf_op jit(solution)/shard_map/ppermute | solution.py:19
  432.3 6.0 %collective-permute-done.43 = f32[1,16,256]{2,1,0:T(8,128)S(1)} collective-permute-done((f32[1,16,256]{2,1,0:T(8,128)S(1)}, f32[1,16,256]{2,1,0:T(8,128)S(1)}, u32[]{:S(2)}, u32[]{:S(2)}) %collective-permute-start.43) | collective-permute-done | bytes 16416 | tf_op jit(solution)/shard_map/ppermute | solution.py:19
  440.2 5.4 %collective-permute-start.45 = (f32[10,1,256]{2,1,0:T(1,128)S(1)}, f32[10,1,256]{2,1,0:T(1,128)S(1)}, u32[]{:S(2)}, u32[]{:S(2)}) collective-permute-start(f32[10,1,256]{2,1,0:T(1,128)S(1)} %get-tuple-element.43), channel_id=1, source_target_pairs={{0,1},{1,2},{2,3},{3,4},{4,5},{5,6},{6,7},{8,9},{9,10},{10,11},{11... | collective-permute-start | bytes 30728 | tf_op jit(solution)/shard_map/ppermute | solution.py:19
  452.6 6.0 %collective-permute-done.47 = f32[1,16,256]{2,1,0:T(8,128)S(1)} collective-permute-done((f32[1,16,256]{2,1,0:T(8,128)S(1)}, f32[1,16,256]{2,1,0:T(8,128)S(1)}, u32[]{:S(2)}, u32[]{:S(2)}) %collective-permute-start.47) | collective-permute-done | bytes 16416 | tf_op jit(solution)/shard_map/ppermute | solution.py:19
  460.5 5.4 %collective-permute-start.49 = (f32[10,1,256]{2,1,0:T(1,128)S(1)}, f32[10,1,256]{2,1,0:T(1,128)S(1)}, u32[]{:S(2)}, u32[]{:S(2)}) collective-permute-start(f32[10,1,256]{2,1,0:T(1,128)S(1)} %get-tuple-element.41), channel_id=1, source_target_pairs={{0,1},{1,2},{2,3},{3,4},{4,5},{5,6},{6,7},{8,9},{9,10},{10,11},{11... | collective-permute-start | bytes 30728 | tf_op jit(solution)/shard_map/ppermute | solution.py:19
  (247 shorter events, 135.7 us)
Async XLA Ops:
  0.8 8.9 %collective-permute-start.1 = (f32[2,16,256]{2,1,0:T(8,128)S(1)}, f32[2,16,256]{2,1,0:T(8,128)S(1)}, u32[]{:S(2)}, u32[]{:S(2)}) collective-permute-start(f32[2,16,256]{2,1,0:T(8,128)S(1)} %get-tuple-element.56), channel_id=1, source_target_pairs={{0,8},{8,16},{16,24},{24,32},{32,40},{40,48},{48,56},{56,64},{64,7... | collective-permute-start | bytes 98312 | tf_op jit(solution)/shard_map/ppermute | solution.py:19
  2.7 8.5 %collective-permute-start = (f32[2,16,256]{2,1,0:T(8,128)S(1)}, f32[2,16,256]{2,1,0:T(8,128)S(1)}, u32[]{:S(2)}, u32[]{:S(2)}) collective-permute-start(f32[2,16,256]{2,1,0:T(8,128)S(1)} %get-tuple-element.57), channel_id=1, source_target_pairs={{8,0},{16,8},{24,16},{32,24},{40,32},{48,40},{56,48},{64,56},{72,6... | collective-permute-start | bytes 98312 | tf_op jit(solution)/shard_map/ppermute | solution.py:20
  11.3 7.4 %collective-permute-start.2 = (f32[12,2,256]{2,1,0:T(2,128)S(1)}, f32[12,2,256]{2,1,0:T(2,128)S(1)}, u32[]{:S(2)}, u32[]{:S(2)}) collective-permute-start(f32[12,2,256]{2,1,0:T(2,128)S(1)} %get-tuple-element.39), channel_id=1, source_target_pairs={{1,0},{2,1},{3,2},{4,3},{5,4},{6,5},{7,6},{9,8},{10,9},{11,10},{12... | collective-permute-start | bytes 73736 | tf_op jit(solution)/shard_map/ppermute | solution.py:20
  21.6 22.8 %collective-permute-start.4 = (f32[1,16,256]{2,1,0:T(8,128)S(1)}, f32[1,16,256]{2,1,0:T(8,128)S(1)}, u32[]{:S(2)}, u32[]{:S(2)}) collective-permute-start(f32[1,16,256]{2,1,0:T(8,128)S(1)} %get-tuple-element.55), channel_id=1, source_target_pairs={{8,0},{16,8},{24,16},{32,24},{40,32},{48,40},{56,48},{64,56},{72,6... | collective-permute-start | bytes 49160 | tf_op jit(solution)/shard_map/ppermute | solution.py:20
  27.8 16.6 %collective-permute-start.5 = (f32[1,16,256]{2,1,0:T(8,128)S(1)}, f32[1,16,256]{2,1,0:T(8,128)S(1)}, u32[]{:S(2)}, u32[]{:S(2)}) collective-permute-start(f32[1,16,256]{2,1,0:T(8,128)S(1)} %get-tuple-element.54), channel_id=1, source_target_pairs={{0,8},{8,16},{16,24},{24,32},{32,40},{40,48},{48,56},{56,64},{64,7... | collective-permute-start | bytes 49160 | tf_op jit(solution)/shard_map/ppermute | solution.py:19
  53.1 18.1 %collective-permute-start.8 = (f32[1,16,256]{2,1,0:T(8,128)S(1)}, f32[1,16,256]{2,1,0:T(8,128)S(1)}, u32[]{:S(2)}, u32[]{:S(2)}) collective-permute-start(f32[1,16,256]{2,1,0:T(8,128)S(1)} %get-tuple-element.53), channel_id=1, source_target_pairs={{8,0},{16,8},{24,16},{32,24},{40,32},{48,40},{56,48},{64,56},{72,6... | collective-permute-start | bytes 49160 | tf_op jit(solution)/shard_map/ppermute | solution.py:20
  59.2 12.0 %collective-permute-start.9 = (f32[1,16,256]{2,1,0:T(8,128)S(1)}, f32[1,16,256]{2,1,0:T(8,128)S(1)}, u32[]{:S(2)}, u32[]{:S(2)}) collective-permute-start(f32[1,16,256]{2,1,0:T(8,128)S(1)} %get-tuple-element.52), channel_id=1, source_target_pairs={{0,8},{8,16},{16,24},{24,32},{32,40},{40,48},{48,56},{56,64},{64,7... | collective-permute-start | bytes 49160 | tf_op jit(solution)/shard_map/ppermute | solution.py:19
  61.1 17.2 %collective-permute-start.12 = (f32[2,8,128]{2,1,0:T(8,128)S(1)}, f32[2,8,128]{2,1,0:T(8,128)S(1)}, u32[]{:S(2)}, u32[]{:S(2)}) collective-permute-start(f32[2,8,128]{2,1,0:T(8,128)S(1)} %get-tuple-element.91), channel_id=1, source_target_pairs={{8,0},{16,8},{24,16},{32,24},{40,32},{48,40},{56,48},{64,56},{72,6... | collective-permute-start | bytes 24584 | tf_op jit(solution)/shard_map/ppermute | solution.py:20
  68.1 10.2 %collective-permute-start.13 = (f32[2,8,128]{2,1,0:T(8,128)S(1)}, f32[2,8,128]{2,1,0:T(8,128)S(1)}, u32[]{:S(2)}, u32[]{:S(2)}) collective-permute-start(f32[2,8,128]{2,1,0:T(8,128)S(1)} %get-tuple-element.90), channel_id=1, source_target_pairs={{0,8},{8,16},{16,24},{24,32},{32,40},{40,48},{48,56},{56,64},{64,7... | collective-permute-start | bytes 24584 | tf_op jit(solution)/shard_map/ppermute | solution.py:19
  71.2 14.2 %collective-permute-start.10 = (f32[10,1,256]{2,1,0:T(1,128)S(1)}, f32[10,1,256]{2,1,0:T(1,128)S(1)}, u32[]{:S(2)}, u32[]{:S(2)}) collective-permute-start(f32[10,1,256]{2,1,0:T(1,128)S(1)} %get-tuple-element.44), channel_id=1, source_target_pairs={{1,0},{2,1},{3,2},{4,3},{5,4},{6,5},{7,6},{9,8},{10,9},{11,10},{12... | collective-permute-start | bytes 30728 | tf_op jit(solution)/shard_map/ppermute | solution.py:20
  73.2 12.3 %collective-permute-start.11 = (f32[10,1,256]{2,1,0:T(1,128)S(1)}, f32[10,1,256]{2,1,0:T(1,128)S(1)}, u32[]{:S(2)}, u32[]{:S(2)}) collective-permute-start(f32[10,1,256]{2,1,0:T(1,128)S(1)} %get-tuple-element.45), channel_id=1, source_target_pairs={{0,1},{1,2},{2,3},{3,4},{4,5},{5,6},{6,7},{8,9},{9,10},{10,11},{11... | collective-permute-start | bytes 30728 | tf_op jit(solution)/shard_map/ppermute | solution.py:19
  78.4 21.1 %collective-permute-start.14 = (f32[8,2,128]{2,1,0:T(2,128)S(1)}, f32[8,2,128]{2,1,0:T(2,128)S(1)}, u32[]{:S(2)}, u32[]{:S(2)}) collective-permute-start(f32[8,2,128]{2,1,0:T(2,128)S(1)} %get-tuple-element.73), channel_id=1, source_target_pairs={{1,0},{2,1},{3,2},{4,3},{5,4},{6,5},{7,6},{9,8},{10,9},{11,10},{12... | collective-permute-start | bytes 24584 | tf_op jit(solution)/shard_map/ppermute | solution.py:20
  80.3 19.2 %collective-permute-start.15 = (f32[8,2,128]{2,1,0:T(2,128)S(1)}, f32[8,2,128]{2,1,0:T(2,128)S(1)}, u32[]{:S(2)}, u32[]{:S(2)}) collective-permute-start(f32[8,2,128]{2,1,0:T(2,128)S(1)} %get-tuple-element.72), channel_id=1, source_target_pairs={{0,1},{1,2},{2,3},{3,4},{4,5},{5,6},{6,7},{8,9},{9,10},{10,11},{11... | collective-permute-start | bytes 24584 | tf_op jit(solution)/shard_map/ppermute | solution.py:19
  99.6 8.1 %collective-permute-start.16 = (f32[1,8,128]{2,1,0:T(8,128)S(1)}, f32[1,8,128]{2,1,0:T(8,128)S(1)}, u32[]{:S(2)}, u32[]{:S(2)}) collective-permute-start(f32[1,8,128]{2,1,0:T(8,128)S(1)} %get-tuple-element.89), channel_id=1, source_target_pairs={{8,0},{16,8},{24,16},{32,24},{40,32},{48,40},{56,48},{64,56},{72,6... | collective-permute-start | bytes 12296 | tf_op jit(solution)/shard_map/ppermute | solution.py:20
  105.7 8.2 %collective-permute-start.17 = (f32[1,8,128]{2,1,0:T(8,128)S(1)}, f32[1,8,128]{2,1,0:T(8,128)S(1)}, u32[]{:S(2)}, u32[]{:S(2)}) collective-permute-start(f32[1,8,128]{2,1,0:T(8,128)S(1)} %get-tuple-element.88), channel_id=1, source_target_pairs={{0,8},{8,16},{16,24},{24,32},{32,40},{40,48},{48,56},{56,64},{64,7... | collective-permute-start | bytes 12296 | tf_op jit(solution)/shard_map/ppermute | solution.py:19
  114.0 31.5 %collective-permute-start.18 = (f32[6,1,128]{2,1,0:T(1,128)S(1)}, f32[6,1,128]{2,1,0:T(1,128)S(1)}, u32[]{:S(2)}, u32[]{:S(2)}) collective-permute-start(f32[6,1,128]{2,1,0:T(1,128)S(1)} %get-tuple-element.80), channel_id=1, source_target_pairs={{1,0},{2,1},{3,2},{4,3},{5,4},{6,5},{7,6},{9,8},{10,9},{11,10},{12... | collective-permute-start | bytes 9224 | tf_op jit(solution)/shard_map/ppermute | solution.py:20
  115.9 29.6 %collective-permute-start.19 = (f32[6,1,128]{2,1,0:T(1,128)S(1)}, f32[6,1,128]{2,1,0:T(1,128)S(1)}, u32[]{:S(2)}, u32[]{:S(2)}) collective-permute-start(f32[6,1,128]{2,1,0:T(1,128)S(1)} %get-tuple-element.81), channel_id=1, source_target_pairs={{0,1},{1,2},{2,3},{3,4},{4,5},{5,6},{6,7},{8,9},{9,10},{10,11},{11... | collective-permute-start | bytes 9224 | tf_op jit(solution)/shard_map/ppermute | solution.py:19
  145.6 13.5 %collective-permute-start.20 = (f32[1,8,128]{2,1,0:T(8,128)S(1)}, f32[1,8,128]{2,1,0:T(8,128)S(1)}, u32[]{:S(2)}, u32[]{:S(2)}) collective-permute-start(f32[1,8,128]{2,1,0:T(8,128)S(1)} %get-tuple-element.87), channel_id=1, source_target_pairs={{8,0},{16,8},{24,16},{32,24},{40,32},{48,40},{56,48},{64,56},{72,6... | collective-permute-start | bytes 12296 | tf_op jit(solution)/shard_map/ppermute | solution.py:20
  147.6 11.6 %collective-permute-start.21 = (f32[1,8,128]{2,1,0:T(8,128)S(1)}, f32[1,8,128]{2,1,0:T(8,128)S(1)}, u32[]{:S(2)}, u32[]{:S(2)}) collective-permute-start(f32[1,8,128]{2,1,0:T(8,128)S(1)} %get-tuple-element.86), channel_id=1, source_target_pairs={{0,8},{8,16},{16,24},{24,32},{32,40},{40,48},{48,56},{56,64},{64,7... | collective-permute-start | bytes 12296 | tf_op jit(solution)/shard_map/ppermute | solution.py:19
  150.0 16.3 %collective-permute-start.24 = (f32[1,32,64]{2,1,0:T(8,128)S(1)}, f32[1,32,64]{2,1,0:T(8,128)S(1)}, u32[]{:S(2)}, u32[]{:S(2)}) collective-permute-start(f32[1,32,64]{2,1,0:T(8,128)S(1)} %get-tuple-element.70), channel_id=1, source_target_pairs={{8,0},{16,8},{24,16},{32,24},{40,32},{48,40},{56,48},{64,56},{72,6... | collective-permute-start | bytes 24584 | tf_op jit(solution)/shard_map/ppermute | solution.py:20
  156.5 9.8 %collective-permute-start.25 = (f32[1,32,64]{2,1,0:T(8,128)S(1)}, f32[1,32,64]{2,1,0:T(8,128)S(1)}, u32[]{:S(2)}, u32[]{:S(2)}) collective-permute-start(f32[1,32,64]{2,1,0:T(8,128)S(1)} %get-tuple-element.71), channel_id=1, source_target_pairs={{0,8},{8,16},{16,24},{24,32},{32,40},{40,48},{48,56},{56,64},{64,7... | collective-permute-start | bytes 24584 | tf_op jit(solution)/shard_map/ppermute | solution.py:19
  196.2 8.4 %collective-permute-start.27 = (f32[1,32,64]{2,1,0:T(8,128)S(1)}, f32[1,32,64]{2,1,0:T(8,128)S(1)}, u32[]{:S(2)}, u32[]{:S(2)}) collective-permute-start(f32[1,32,64]{2,1,0:T(8,128)S(1)} %get-tuple-element.68), channel_id=1, source_target_pairs={{0,8},{8,16},{16,24},{24,32},{32,40},{40,48},{48,56},{56,64},{64,7... | collective-permute-start | bytes 24584 | tf_op jit(solution)/shard_map/ppermute | solution.py:19
  204.7 58.2 %collective-permute-start.28 = (f32[1,32,64]{2,1,0:T(8,128)S(1)}, f32[1,32,64]{2,1,0:T(8,128)S(1)}, u32[]{:S(2)}, u32[]{:S(2)}) collective-permute-start(f32[1,32,64]{2,1,0:T(8,128)S(1)} %get-tuple-element.67), channel_id=1, source_target_pairs={{8,0},{16,8},{24,16},{32,24},{40,32},{48,40},{56,48},{64,56},{72,6... | collective-permute-start | bytes 24584 | tf_op jit(solution)/shard_map/ppermute | solution.py:20
  206.7 56.2 %collective-permute-start.29 = (f32[1,32,64]{2,1,0:T(8,128)S(1)}, f32[1,32,64]{2,1,0:T(8,128)S(1)}, u32[]{:S(2)}, u32[]{:S(2)}) collective-permute-start(f32[1,32,64]{2,1,0:T(8,128)S(1)} %get-tuple-element.66), channel_id=1, source_target_pairs={{0,8},{8,16},{16,24},{24,32},{32,40},{40,48},{48,56},{56,64},{64,7... | collective-permute-start | bytes 24584 | tf_op jit(solution)/shard_map/ppermute | solution.py:19
  363.9 8.4 %collective-permute-start.31 = (f32[1,32,64]{2,1,0:T(8,128)S(1)}, f32[1,32,64]{2,1,0:T(8,128)S(1)}, u32[]{:S(2)}, u32[]{:S(2)}) collective-permute-start(f32[1,32,64]{2,1,0:T(8,128)S(1)} %get-tuple-element.64), channel_id=1, source_target_pairs={{0,8},{8,16},{16,24},{24,32},{32,40},{40,48},{48,56},{56,64},{64,7... | collective-permute-start | bytes 24584 | tf_op jit(solution)/shard_map/ppermute | solution.py:19
  375.2 8.4 %collective-permute-start.33 = (f32[1,32,64]{2,1,0:T(8,128)S(1)}, f32[1,32,64]{2,1,0:T(8,128)S(1)}, u32[]{:S(2)}, u32[]{:S(2)}) collective-permute-start(f32[1,32,64]{2,1,0:T(8,128)S(1)} %get-tuple-element.61), channel_id=1, source_target_pairs={{0,8},{8,16},{16,24},{24,32},{32,40},{40,48},{48,56},{56,64},{64,7... | collective-permute-start | bytes 24584 | tf_op jit(solution)/shard_map/ppermute | solution.py:19
  388.3 8.2 %collective-permute-start.35 = (f32[1,8,128]{2,1,0:T(8,128)S(1)}, f32[1,8,128]{2,1,0:T(8,128)S(1)}, u32[]{:S(2)}, u32[]{:S(2)}) collective-permute-start(f32[1,8,128]{2,1,0:T(8,128)S(1)} %get-tuple-element.84), channel_id=1, source_target_pairs={{0,8},{8,16},{16,24},{24,32},{32,40},{40,48},{48,56},{56,64},{64,7... | collective-permute-start | bytes 12296 | tf_op jit(solution)/shard_map/ppermute | solution.py:19
  408.8 8.2 %collective-permute-start.39 = (f32[1,8,128]{2,1,0:T(8,128)S(1)}, f32[1,8,128]{2,1,0:T(8,128)S(1)}, u32[]{:S(2)}, u32[]{:S(2)}) collective-permute-start(f32[1,8,128]{2,1,0:T(8,128)S(1)} %get-tuple-element.82), channel_id=1, source_target_pairs={{0,8},{8,16},{16,24},{24,32},{32,40},{40,48},{48,56},{56,64},{64,7... | collective-permute-start | bytes 12296 | tf_op jit(solution)/shard_map/ppermute | solution.py:19
  429.9 8.4 %collective-permute-start.43 = (f32[1,16,256]{2,1,0:T(8,128)S(1)}, f32[1,16,256]{2,1,0:T(8,128)S(1)}, u32[]{:S(2)}, u32[]{:S(2)}) collective-permute-start(f32[1,16,256]{2,1,0:T(8,128)S(1)} %get-tuple-element.50), channel_id=1, source_target_pairs={{0,8},{8,16},{16,24},{24,32},{32,40},{40,48},{48,56},{56,64},{64,7... | collective-permute-start | bytes 49160 | tf_op jit(solution)/shard_map/ppermute | solution.py:19
  438.3 7.3 %collective-permute-start.44 = (f32[10,1,256]{2,1,0:T(1,128)S(1)}, f32[10,1,256]{2,1,0:T(1,128)S(1)}, u32[]{:S(2)}, u32[]{:S(2)}) collective-permute-start(f32[10,1,256]{2,1,0:T(1,128)S(1)} %get-tuple-element.42), channel_id=1, source_target_pairs={{1,0},{2,1},{3,2},{4,3},{5,4},{6,5},{7,6},{9,8},{10,9},{11,10},{12... | collective-permute-start | bytes 30728 | tf_op jit(solution)/shard_map/ppermute | solution.py:20
  450.2 8.4 %collective-permute-start.47 = (f32[1,16,256]{2,1,0:T(8,128)S(1)}, f32[1,16,256]{2,1,0:T(8,128)S(1)}, u32[]{:S(2)}, u32[]{:S(2)}) collective-permute-start(f32[1,16,256]{2,1,0:T(8,128)S(1)} %get-tuple-element.48), channel_id=1, source_target_pairs={{0,8},{8,16},{16,24},{24,32},{32,40},{40,48},{48,56},{56,64},{64,7... | collective-permute-start | bytes 49160 | tf_op jit(solution)/shard_map/ppermute | solution.py:19
  458.6 7.3 %collective-permute-start.48 = (f32[10,1,256]{2,1,0:T(1,128)S(1)}, f32[10,1,256]{2,1,0:T(1,128)S(1)}, u32[]{:S(2)}, u32[]{:S(2)}) collective-permute-start(f32[10,1,256]{2,1,0:T(1,128)S(1)} %get-tuple-element.40), channel_id=1, source_target_pairs={{1,0},{2,1},{3,2},{4,3},{5,4},{6,5},{7,6},{9,8},{10,9},{11,10},{12... | collective-permute-start | bytes 30728 | tf_op jit(solution)/shard_map/ppermute | solution.py:20
  (54 other events, 2716.6 us)
where the time goes:
time: 471 us; the launch traced here: 468 us
  starting transfers between devices  163 us (35%)
  blocking collectives  151 us (32%)
  waiting for transfers between devices  59.3 us (13%)
  other arithmetic  51.5 us (11%)
  local copies, waits for them, and re-layouts  30.4 us (6%)
  between operations  13.2 us (3%)
    ppermute x25, starting transfers between devices, with_halo(): before = lax.ppermute(last, axis, up)  83 us
    ppermute x25, starting transfers between devices, with_halo(): after = lax.ppermute(leading, axis, down)  79.8 us
    ppermute x25, waiting for transfers between devices, with_halo(): before = lax.ppermute(last, axis, up)  58.6 us
    all_gather x1, blocking collectives, per_device(): lax.all_gather(k3, 'wide', axis=0, tiled=True)  53.8 us
    all_gather x1, blocking collectives, per_device(): lax.all_gather(r3, 'wide', axis=0, tiled=True)  48 us
    all_gather x1, blocking collectives, per_device(): lax.all_gather(r2, 'narrow', axis=1, tiled=True)  24.7 us
    all_gather x1, blocking collectives, per_device(): lax.all_gather(k2, 'narrow', axis=1, tiled=True)  24.5 us
    reduce_sum x5, other arithmetic, coarse_solve(): alpha = norm_now / jnp.sum(direction * image)  16.3 us
  transfers between devices with their start and end apart: 50, of which 16 were waited for; matrix products, arithmetic and copies ran while one was open for 7% of the time, Pallas kernels for 0%

commit v1 on v0

v1 whole, which is shorter than its diff:
```python
import functools

import jax
import jax.numpy as jnp
from jax import lax
from jax.experimental import pallas as pl
from jax.experimental.pallas import tpu as pltpu
from jax.sharding import PartitionSpec as P

COARSE_ITERS = 5
OMEGA = 0.8
MESH = pl.DeviceIdType.MESH
F32 = jnp.float32

OWN = 7
PLANES = 22
HALO_K, HALO_R = 7, 6
OWN1 = 3
PLANES1 = 10


def split(x):
    high = x.astype(jnp.bfloat16)
    rest = x - high.astype(F32)
    middle = rest.astype(jnp.bfloat16)
    low = (rest - middle.astype(F32)).astype(jnp.bfloat16)
    return high, middle, low


def times_right(x, zero_one):
    rows = x.shape[0]
    out = jnp.dot(jnp.concatenate(split(x), axis=0), zero_one, preferred_element_type=F32)
    return out[:rows] + out[rows : 2 * rows] + out[2 * rows :]


def times_left(zero_one, x):
    columns = x.shape[1]
    out = jnp.dot(zero_one, jnp.concatenate(split(x), axis=1), preferred_element_type=F32)
    return out[:, :columns] + out[:, columns : 2 * columns] + out[:, 2 * columns :]


def iotas(rows, columns):
    shape = (rows, columns)
    return lax.broadcasted_iota(jnp.int32, shape, 0), lax.broadcasted_iota(jnp.int32, shape, 1)


def zero_one(condition):
    return jnp.where(condition, 1.0, 0.0).astype(jnp.bfloat16)


def halve_z():
    fine, coarse = iotas(256, 128)
    return zero_one(fine // 2 == coarse)


def double_z():
    coarse, fine = iotas(128, 256)
    return zero_one(fine // 2 == coarse)


def weights(first, last, k, wx, wy, wz, diag, inv):
    rows, columns = k.shape[1:]
    lane = lax.broadcasted_iota(jnp.int32, (rows, columns), 1)
    rim = jnp.where((lane == 0) | (lane == columns - 1), 0.5, 0.0)
    half = jnp.where(lane == columns - 1, 0.0, 0.5)
    wx[first - 1] = 0.5 * (k[first - 1] + k[first])

    def plane(p):
        here = k[p]
        x = 0.5 * (here + k[p + 1])
        y = 0.5 * (here + pltpu.roll(here, rows - 1, 0))
        z = half * (here + pltpu.roll(here, columns - 1, 1))
        d = (x + wx[p - 1]) + (y + pltpu.roll(y, 1, 0)) + (z + pltpu.roll(z, 1, 1)) + rim * here
        wx[p] = x
        wy[p] = y
        wz[p] = z
        diag[p] = d
        inv[p] = jnp.where(here > 0.0, OMEGA / d, 0.0)

    return plane


def image_at(p, v, wx, wy, wz, diag):
    rows, columns = v.shape[1:]
    here = v[p]
    y, z = wy[p], wz[p]
    total = wx[p] * v[p + 1] + wx[p - 1] * v[p - 1]
    total += y * pltpu.roll(here, rows - 1, 0) + pltpu.roll(y * here, 1, 0)
    total += z * pltpu.roll(here, columns - 1, 1) + pltpu.roll(z * here, 1, 1)
    return diag[p] * here - total


def loop(first, last, body, unroll):
    if unroll:
        for p in range(first, last):
            body(p)
    else:

        def step(p, carry):
            body(p)
            return carry

        lax.fori_loop(first, last, step, 0)


def corner_pack(k, r, x_low, y_low):
    sub = lax.broadcasted_iota(jnp.int32, (8, 256), 0)
    near = 7 - sub if y_low else sub
    turn = lambda x, by: pltpu.roll(x, (by if y_low else -by) % 8, 0)
    return [
        jnp.where(near < 6, k(1), turn(k(5), 2)),
        jnp.where(near < 5, k(2), turn(r(3), 3)),
        jnp.where(near < 4, k(3), turn(r(2), 4)),
        jnp.where(near < 5, r(1), turn(k(4), 3)),
        jnp.where(near < 2, r(4), jnp.where(near == 2, turn(r(5), -2), turn(k(6), -3))),
    ]


def corner_unpack(tiles, y_low):
    turn = lambda x, by: pltpu.roll(x, (by if y_low else -by) % 8, 0)
    one, two, three, four, five = tiles
    k = [one, two, three, turn(four, -3), turn(one, -2), turn(five, 3)]
    r = [four, turn(three, -4), turn(two, -3), five, turn(five, 2)]
    return k, r


def kernel(nw, nn, r_in, k_in, out, *refs):
    (K0, R0, EA, EB, WX, WY, WZ, DG, IV, XS, CS, CR, T0,
     K1, R1, A1, B1, WX1, WY1, WZ1, DG1, IV1, E1S, E1G, T1,
     SB2, G2, KS, GK, K2X, K2S, K3S, K3G, R3S, R3G, F3,
     X3, Y3, Z3, D3, S3, Q3, P3, MB, E2G, E3, DS,
     load, halo_s, halo_r, kz_s, kz_r, rz_s, rz_r, kx_s, kx_r, e1_s, e1_r,
     k3_s, k3_r, r3_s, r3_r, e2_s, e2_r) = refs
    w, n = lax.axis_index("wide"), lax.axis_index("narrow")
    wide = lambda d: lax.rem(w + (d + nw), nw)
    narrow = lambda d: lax.rem(n + (d + nn), nn)

    def outside(dx, dy):
        over = jnp.int32(0)
        if dx:
            over = over + jnp.where(w == (nw - 1 if dx > 0 else 0), 1, 0)
            if abs(dx) == 2:
                over = over + jnp.where(w == (nw - 2 if dx > 0 else 1), 1, 0)
        if dy:
            over = over + jnp.where(n == (nn - 1 if dy > 0 else 0), 1, 0)
        return jnp.where(over > 0, 1, 0)

    def remote(src, dst, send, recv, to):
        return pltpu.make_async_remote_copy(
            src_ref=src, dst_ref=dst, send_sem=send, recv_sem=recv, device_id=to, device_id_type=MESH
        )

    load_k = pltpu.make_async_copy(k_in, K0.at[OWN : OWN + 8, 0:16], load.at[0])
    load_r = pltpu.make_async_copy(r_in, R0.at[OWN : OWN + 8, 0:16], load.at[1])
    load_k.start()
    load_r.start()
    barrier = pltpu.get_barrier_semaphore()

    def greet_wide(d, carry):
        pl.semaphore_signal(barrier, inc=1, device_id=(wide(d), n), device_id_type=MESH)
        return carry

    def greet_narrow(d, carry):
        for dx in (-1, 0, 1):
            pl.semaphore_signal(barrier, inc=1, device_id=(wide(dx), narrow(d)), device_id_type=MESH)
        return carry

    lax.fori_loop(1, nn, greet_narrow, 0)
    lax.fori_loop(1, nw, greet_wide, 0)

    zero_planes = jnp.zeros((8, 16, 256), F32)
    K0[PLANES : PLANES + 8, 0:16] = zero_planes
    R0[PLANES : PLANES + 8, 0:16] = zero_planes
    zero_rows = jnp.zeros((16, 256), F32)
    for p in (0, 21):
        K0[p, 16:32] = zero_rows
    for p in (1, 20):
        R0[p, 16:32] = zero_rows
    SB2[1] = jnp.zeros((4, 128), F32)
    K2X[1] = jnp.zeros((32, 128), F32)
    MB[1] = jnp.zeros((2, 32, 128), F32)
    E1S[1] = jnp.zeros((4, 3, 8, 128), F32)
    E3[...] = jnp.zeros((4, nw + 16, 128), F32)
    load_k.wait()
    load_r.wait()

    corners = [(dx, dy) for dx in (-1, 1) for dy in (-1, 1)]
    for i, (dx, dy) in enumerate(corners):
        rows = pl.ds(8, 8) if dy > 0 else pl.ds(0, 8)
        at = lambda a: OWN + (8 - a if dx > 0 else a - 1)
        keep = jnp.where(outside(dx, dy) == 0, 1.0, 0.0).astype(F32)
        tiles = corner_pack(lambda a: K0[at(a), rows], lambda a: R0[at(a), rows], dx > 0, dy > 0)
        for t, tile in enumerate(tiles):
            CS[i, t] = tile * keep

    fine, coarse = iotas(512, 128)
    to_quarter = zero_one(((fine // 256) == (coarse // 64)) & ((fine % 256) // 4 == coarse % 64))
    parts = [
        (K0[OWN + 4 * p, 0:16] + K0[OWN + 4 * p + 1, 0:16]) + (K0[OWN + 4 * p + 2, 0:16] + K0[OWN + 4 * p + 3, 0:16])
        for p in (0, 1)
    ]
    T0[0:16] = times_right(jnp.concatenate(parts, axis=1), to_quarter)
    quarter = (T0[pl.ds(0, 4, stride=4)] + T0[pl.ds(1, 4, stride=4)]) + (
        T0[pl.ds(2, 4, stride=4)] + T0[pl.ds(3, 4, stride=4)]
    )
    KS[...] = quarter * (1.0 / 64.0)

    pl.semaphore_wait(barrier, (nw - 1) + 3 * (nn - 1))

    halo = []

    def push(src, dst, to):
        i = len(halo)
        halo.append(remote(src, dst, halo_s.at[i], halo_r.at[i], to))
        halo[-1].start()

    for dx in (-1, 1):
        over = outside(dx, 0)
        for ref, width in ((K0, HALO_K), (R0, HALO_R)):
            start = OWN + 8 - width if dx > 0 else OWN
            land = OWN - width if dx > 0 else OWN + 8
            start = jnp.where(over == 1, PLANES, start)
            push(ref.at[pl.ds(start, width), 0:16], ref.at[land : land + width, 0:16], (wide(dx), n))
    for dy in (-1, 1):
        over = outside(0, dy)
        for ref in (K0, R0):
            start = jnp.where(over == 1, PLANES, OWN)
            rows = slice(8, 16) if dy > 0 else slice(0, 8)
            land = slice(24, 32) if dy > 0 else slice(16, 24)
            push(ref.at[pl.ds(start, 8), rows], ref.at[OWN : OWN + 8, land], (w, narrow(dy)))
    for i, (dx, dy) in enumerate(corners):
        push(CS.at[i], CR.at[3 - i], (wide(dx), narrow(dy)))

    def gather_k(d, carry):
        remote(KS, GK.at[n], kz_s.at[0], kz_r.at[0], (w, narrow(d))).start()
        return carry

    lax.fori_loop(1, nn, gather_k, 0)
    GK[n] = KS[...]

    for copy in halo:
        copy.wait_recv()
    for i, (dx, dy) in enumerate(corners):
        k, r = corner_unpack([CR[i, t] for t in range(5)], dy < 0)
        rows = pl.ds(24, 8) if dy < 0 else pl.ds(16, 8)
        at = lambda a: OWN - a if dx < 0 else OWN + 7 + a
        for a in range(1, 7):
            K0[at(a), rows] = k[a - 1]
        for a in range(1, 6):
            R0[at(a), rows] = r[a - 1]

    level0 = (WX, WY, WZ, DG)
    set_weights = weights(1, 21, K0, WX, WY, WZ, DG, IV)

    def first0(p):
        set_weights(p)
        EA[p] = IV[p] * R0[p]

    loop(1, 21, first0, False)

    def sweep0(source, target):
        def plane(p):
            target[p] = source[p] + IV[p] * (R0[p] - image_at(p, source, *level0))

        return plane

    loop(2, 20, sweep0(EA, EB), False)

    def residual0(i):
        p = 2 * i + 3
        XS[i] = (R0[p] - image_at(p, EB, *level0)) + (R0[p + 1] - image_at(p + 1, EB, *level0))

    loop(0, 8, residual0, False)
    halve = halve_z()
    T0[0:256] = times_right(XS[...].reshape(256, 256), halve)
    R1[1:9] = (0.5 * (T0[pl.ds(0, 128, stride=2)] + T0[pl.ds(1, 128, stride=2)])).reshape(8, 16, 128)
    k_pairs = jnp.concatenate([K0[2 * q + 1] + K0[2 * q + 2] for q in range(PLANES1)], axis=0)
    T0[...] = times_right(k_pairs, halve)
    K1[...] = (0.125 * (T0[pl.ds(0, 160, stride=2)] + T0[pl.ds(1, 160, stride=2)])).reshape(PLANES1, 16, 128)

    level1 = (WX1, WY1, WZ1, DG1)
    set_weights1 = weights(1, 9, K1, WX1, WY1, WZ1, DG1, IV1)

    def first1(q):
        set_weights1(q)
        A1[q] = IV1[q] * R1[q]

    def sweep1(source, target):
        def plane(q):
            target[q] = source[q] + IV1[q] * (R1[q] - image_at(q, source, *level1))

        return plane

    loop(1, 9, first1, True)
    loop(2, 8, sweep1(A1, B1), True)
    left = [R1[q] - image_at(q, B1, *level1) for q in range(OWN1, OWN1 + 4)]
    fine, coarse = iotas(256, 128)
    halve_pair = zero_one(((fine // 128) == (coarse // 64)) & ((fine % 128) // 2 == coarse % 64))
    pair = jnp.concatenate([(left[0] + left[1])[0:8], (left[2] + left[3])[0:8]], axis=1)
    pair = jnp.concatenate([pair, pair], axis=0)
    T0[0:16] = times_right(pair, halve_pair)
    SB2[0] = 0.5 * (T0[pl.ds(0, 4, stride=2)] + T0[pl.ds(1, 4, stride=2)])

    def gather_r(d, carry):
        for dx in (-1, 0, 1):
            src = SB2.at[outside(dx, 0)]
            remote(src, G2.at[(1 - dx) * nn + n], rz_s.at[0], rz_r.at[0], (wide(dx), narrow(d))).start()
        return carry

    lax.fori_loop(1, nn, gather_r, 0)
    for dx in (-1, 1):
        remote(SB2.at[outside(dx, 0)], G2.at[(1 - dx) * nn + n], rz_s.at[0], rz_r.at[0], (wide(dx), n)).start()
    G2[nn + n] = SB2[0]

    for x1 in range(4):
        E1S[0, x1, 0] = B1[OWN1 + x1, 0:8]
        E1S[0, x1, 1] = R1[OWN1 + x1, 0:8]
        E1S[0, x1, 2] = K1[OWN1 + x1, 0:8]
    around = [(dx, dy) for dx in (-1, 0, 1) for dy in (-1, 0, 1) if dx or dy]
    near = []
    for i, (dx, dy) in enumerate(around):
        src, dst = E1S.at[outside(dx, dy)], E1G.at[7 - i]
        planes = slice(1, 4) if dx > 0 else (slice(0, 3) if dx < 0 else slice(0, 4))
        arrays = slice(0, 3) if dx and dy else slice(0, 1)
        src, dst = src.at[planes, arrays], dst.at[planes, arrays]
        copy = remote(src, dst, e1_s.at[i], e1_r.at[i], (wide(dx), narrow(dy)))
        copy.start()
        near.append(copy)

    remote(GK.at[0 : nn - 1], GK.at[0 : nn - 1], kz_s.at[0], kz_r.at[0], (w, n)).wait_recv()
    for i in range(nn):
        K2X[0, 4 * i : 4 * i + 4] = GK[i]
    slab_k = K2X[0]
    beside = (-2, -1, 1, 2)
    kx = []
    for i, dx in enumerate(beside):
        copy = remote(K2X.at[outside(dx, 0)], K2S.at[2 - dx], kx_s.at[i], kx_r.at[i], (wide(dx), n))
        copy.start()
        kx.append(copy)
    K2S[2] = slab_k

    row, lane = iotas(32, 128)
    own_chunk = (row // 8) == (lane // 32)
    fine, coarse = iotas(128, 128)
    fold = zero_one((fine % 64) // 2 == coarse % 32)
    unfold = zero_one((coarse % 64) // 2 == fine % 32)

    def to_level3(x):
        spread = jnp.where(own_chunk, times_right(x, fold), 0.0)
        T1[...] = (spread[0:8] + spread[8:16]) + (spread[16:24] + spread[24:32])
        return T1[pl.ds(0, 4, stride=2)] + T1[pl.ds(1, 4, stride=2)]

    def to_all(src, dst, send, recv):
        def one(d, carry):
            remote(src, dst.at[w], send.at[0], recv.at[0], (wide(d), n)).start()
            return carry

        lax.fori_loop(1, nw, one, 0)
        dst[w] = src[...]

    def from_all(dst, send, recv):
        return remote(dst.at[0 : nw - 1], dst.at[0 : nw - 1], send.at[0], recv.at[0], (w, n))

    K3S[...] = 0.125 * to_level3(slab_k)
    to_all(K3S, K3G, k3_s, k3_r)

    for copy in kx:
        copy.wait_recv()
    k2 = K2S[...]
    row = lax.broadcasted_iota(jnp.int32, (5, 32, 128), 1)
    cell = lax.broadcasted_iota(jnp.int32, (5, 32, 128), 2)
    odd = cell >= 64
    cell = cell % 64
    none = jnp.zeros((1, 32, 128), F32)

    def above(v):
        turned = pltpu.roll(v, 64, 2)
        after = jnp.concatenate([turned[1:], none], axis=0)
        return jnp.where(odd[: v.shape[0]], after, turned)

    def below(v):
        turned = pltpu.roll(v, 64, 2)
        before = jnp.concatenate([none, turned[:-1]], axis=0)
        return jnp.where(odd[: v.shape[0]], turned, before)

    wx2 = 0.5 * (k2 + above(k2))
    wy2 = jnp.where(row == 31, 0.0, 0.5 * (k2 + pltpu.roll(k2, 31, 1)))
    wz2 = jnp.where(cell == 63, 0.0, 0.5 * (k2 + pltpu.roll(k2, 127, 2)))
    diag2 = (wx2 + below(wx2)) + (wy2 + pltpu.roll(wy2, 1, 1)) + (wz2 + pltpu.roll(wz2, 1, 2))
    diag2 += jnp.where((row == 0) | (row == 31), 0.5 * k2, 0.0) + jnp.where((cell == 0) | (cell == 63), 0.5 * k2, 0.0)
    inv2 = jnp.where(k2 > 0.0, OMEGA / diag2, 0.0)

    def image2(v, at):
        x, y, z = wx2[at], wy2[at], wz2[at]
        total = x * above(v) + below(x * v)
        total += y * pltpu.roll(v, 31, 1) + pltpu.roll(y * v, 1, 1)
        total += z * pltpu.roll(v, 127, 2) + pltpu.roll(z * v, 1, 2)
        return diag2[at] * v - total

    some = slice(1, 4)
    arrived = G2.at[0 : 3 * nn - 1]
    remote(arrived, arrived, rz_s.at[0], rz_r.at[0], (w, n)).wait_recv()
    r2 = jnp.concatenate(
        [jnp.concatenate([G2[b * nn + i] for i in range(nn)], axis=0)[None] for b in range(3)], axis=0
    )
    e2 = inv2[some] * r2
    e2 = e2 + inv2[some] * (r2 - image2(e2, some))
    left2 = (r2 - image2(e2, some))[1]
    R3S[...] = 0.5 * to_level3(left2)
    to_all(R3S, R3G, r3_s, r3_r)

    MB[0, 0] = e2[1]
    MB[0, 1] = r2[1]
    e2x = []
    for i, dx in enumerate(beside):
        copy = remote(MB.at[outside(dx, 0)], E2G.at[2 - dx], e2_s.at[i], e2_r.at[i], (wide(dx), n))
        copy.start()
        e2x.append(copy)
    E2G[2] = MB[0]

    for copy in near:
        copy.wait_recv()
    sub = lax.broadcasted_iota(jnp.int32, (8, 128), 0)

    def rim1(x1, which):
        dx = -1 if x1 < 0 else (1 if x1 > 3 else 0)
        after, before = around.index((dx, 1)), around.index((dx, -1))
        return jnp.where(sub < 4, E1G[after, x1 - 4 * dx, which], E1G[before, x1 - 4 * dx, which])

    for x1 in (-3, -2, -1, 4, 5, 6):
        K1[OWN1 + x1, 8:16] = rim1(x1, 2)
        if -2 <= x1 <= 5:
            R1[OWN1 + x1, 8:16] = rim1(x1, 1)
    loop(1, 9, set_weights1, True)

    from_all(K3G, k3_s, k3_r).wait_recv()

    def in_order(gathered, target):
        for i in range(nw):
            F3[4 * i : 4 * i + 4] = gathered[i]
        for j in range(4):
            target[j] = F3[pl.ds(j, nw, stride=4)]

    in_order(K3G, P3)
    row, lane = iotas(nw, 128)
    last_chunk, first_chunk = lane >= 96, lane < 32
    for j in range(4):
        here = P3[j]
        X3[j] = jnp.where(row == nw - 1, 0.0, 0.5 * (here + pltpu.roll(here, nw - 1, 0)))
        Z3[j] = jnp.where(lane % 32 == 31, 0.0, 0.5 * (here + pltpu.roll(here, 127, 1)))
        if j < 3:
            Y3[j] = 0.5 * (here + P3[j + 1])
        else:
            Y3[j] = jnp.where(last_chunk, 0.0, 0.5 * (here + pltpu.roll(P3[0], 96, 1)))
    for j in range(4):
        here = P3[j]
        lower = Y3[j - 1] if j else pltpu.roll(Y3[3], 32, 1)
        d = (X3[j] + pltpu.roll(X3[j], 1, 0)) + (Y3[j] + lower) + (Z3[j] + pltpu.roll(Z3[j], 1, 1))
        rim = jnp.where((row == 0) | (row == nw - 1), 0.5, 0.0)
        rim += jnp.where((lane % 32 == 0) | (lane % 32 == 31), 0.5, 0.0)
        if j == 0:
            rim += jnp.where(first_chunk, 0.5, 0.0)
        if j == 3:
            rim += jnp.where(last_chunk, 0.5, 0.0)
        D3[j] = d + rim * here

    from_all(R3G, r3_s, r3_r).wait_recv()
    in_order(R3G, Q3)
    norm = jnp.zeros((nw, 128), F32)
    for j in range(4):
        P3[j] = Q3[j]
        S3[j] = jnp.zeros((nw, 128), F32)
        norm += Q3[j] * Q3[j]
    norm = jnp.sum(norm, keepdims=True)

    def iteration(step, norm):
        images = []
        dot = jnp.zeros((nw, 128), F32)
        carried = pltpu.roll(Y3[3] * P3[3], 32, 1)
        for j in range(4):
            v = P3[j]
            x, y, z = X3[j], Y3[j], Z3[j]
            total = x * pltpu.roll(v, nw - 1, 0) + pltpu.roll(x * v, 1, 0)
            total += z * pltpu.roll(v, 127, 1) + pltpu.roll(z * v, 1, 1)
            total += y * (P3[j + 1] if j < 3 else pltpu.roll(P3[0], 96, 1)) + carried
            carried = y * v
            image = D3[j] * v - total
            images.append(image)
            dot += v * image
        alpha = norm / jnp.sum(dot, keepdims=True)
        following = jnp.zeros((nw, 128), F32)
        for j in range(4):
            S3[j] = S3[j] + alpha * P3[j]
            rest = Q3[j] - alpha * images[j]
            Q3[j] = rest
            following += rest * rest
        following = jnp.sum(following, keepdims=True)
        beta = following / norm
        for j in range(4):
            P3[j] = Q3[j] + beta * P3[j]
        return following

    lax.fori_loop(0, COARSE_ITERS, iteration, norm)
    for j in range(4):
        E3[j, 8 : 8 + nw] = S3[j]

    for i in range(5):
        for j in range(4):
            DS[8 * i + 2 * j : 8 * i + 2 * j + 2] = jnp.broadcast_to(E3[j, pl.ds(w + (6 + i), 1)], (2, 128))
    chunk = lax.broadcasted_iota(jnp.int32, (8, 128), 1) // 32
    rows = [jnp.where(chunk == c, DS[8 * i : 8 * i + 8], 0.0) for i in range(5) for c in range(4)]
    added = times_right(jnp.concatenate(rows, axis=0), unfold).reshape(5, 32, 128)
    for copy in e2x:
        copy.wait_recv()
    r2 = E2G[:, 1]
    e2 = E2G[:, 0] + added
    every = slice(0, 5)
    e2 = e2 + inv2 * (r2 - image2(e2, every))
    e2 = e2 + inv2 * (r2 - image2(e2, every))

    coarse, fine = iotas(128, 256)
    double_pair = zero_one(((fine // 128) == (coarse // 64)) & ((fine % 128) // 2 == coarse % 64))
    stretched = times_right(e2[1:4].reshape(96, 128), double_pair)
    i, y2 = iotas(16, 32)
    y1 = 8 * n + jnp.where(i < 12, i, i - 16)
    pick = zero_one((y1 == 2 * y2) | (y1 == 2 * y2 + 1))
    for b in range(3):
        grown = times_left(pick, stretched[32 * b : 32 * b + 32])
        for p in range(2):
            x2 = 2 * (b - 1) + p
            for x1 in (2 * x2, 2 * x2 + 1):
                if -3 <= x1 <= 6:
                    dx = -1 if x1 < 0 else (1 if x1 > 3 else 0)
                    mine = E1G[around.index((dx, 0)), x1 - 4 * dx, 0] if dx else B1[OWN1 + x1, 0:8]
                    rim = rim1(x1, 0)
                    A1[OWN1 + x1, 0:8] = mine + grown[0:8, 128 * p : 128 * p + 128]
                    A1[OWN1 + x1, 8:16] = rim + grown[8:16, 128 * p : 128 * p + 128]
    loop(1, 9, sweep1(A1, B1), True)
    loop(2, 8, sweep1(B1, A1), True)

    stretched = times_right(A1[2:8].reshape(96, 128), double_z())
    i, j = iotas(32, 16)
    twice = zero_one(i // 2 == j)
    for q in range(6):
        grown = times_left(twice, stretched[16 * q : 16 * q + 16])
        for p in (5 + 2 * q, 6 + 2 * q):
            EA[p] = EB[p] + grown
    loop(6, 16, sweep0(EA, EB), False)

    def last(p):
        value = EB[p] + IV[p] * (R0[p] - image_at(p, EB, *level0))
        out[p - OWN] = value[0:16]

    loop(7, 15, last, False)

    for copy in halo + near + kx + e2x:
        copy.wait_send()
    remote(GK.at[0 : nn - 1], GK.at[0 : nn - 1], kz_s.at[0], kz_r.at[0], (w, n)).wait_send()
    remote(arrived, arrived, rz_s.at[0], rz_r.at[0], (w, n)).wait_send()
    from_all(K3G, k3_s, k3_r).wait_send()
    from_all(R3G, r3_s, r3_r).wait_send()


def solution(mesh):
    nw, nn = mesh.shape["wide"], mesh.shape["narrow"]

    def per_device(right_side, coefficient):
        fine = pltpu.VMEM((PLANES, 32, 256), F32)
        with_zeros = pltpu.VMEM((PLANES + 8, 32, 256), F32)
        middle = pltpu.VMEM((PLANES1, 16, 128), F32)
        coarse = pltpu.VMEM((4, nw, 128), F32)
        vmem = lambda *shape: pltpu.VMEM(shape, F32)
        dma = lambda count: pltpu.SemaphoreType.DMA((count,))
        scratch = [with_zeros, with_zeros] + [fine] * 7
        scratch += [vmem(8, 32, 256), vmem(4, 5, 8, 256), vmem(4, 5, 8, 256), vmem(320, 128)]
        scratch += [middle] * 9 + [vmem(2, 4, 3, 8, 128), vmem(8, 4, 3, 8, 128), vmem(8, 128)]
        scratch += [vmem(2, 4, 128), vmem(3 * nn, 4, 128), vmem(4, 128), vmem(nn, 4, 128)]
        scratch += [vmem(2, 32, 128), vmem(5, 32, 128)]
        scratch += [vmem(4, 128), vmem(nw, 4, 128), vmem(4, 128), vmem(nw, 4, 128), vmem(4 * nw, 128)]
        scratch += [coarse] * 7
        scratch += [vmem(2, 2, 32, 128), vmem(5, 2, 32, 128), vmem(4, nw + 16, 128), vmem(40, 128)]
        scratch += [dma(2), dma(12), dma(12), dma(1), dma(1), dma(1), dma(1), dma(4), dma(4), dma(8), dma(8)]
        scratch += [dma(1), dma(1), dma(1), dma(1), dma(4), dma(4)]
        return pl.pallas_call(
            functools.partial(kernel, nw, nn),
            out_shape=jax.ShapeDtypeStruct((8, 16, 256), F32),
            in_specs=[pl.BlockSpec(memory_space=pl.ANY)] * 2,
            out_specs=pl.BlockSpec(memory_space=pltpu.VMEM),
            scratch_shapes=scratch,
            compiler_params=pltpu.CompilerParams(
                collective_id=0, has_side_effects=True, vmem_limit_bytes=40 * 1024 * 1024
            ),
        )(right_side, coefficient)

    placed = P("wide", "narrow", None)
    return jax.shard_map(per_device, mesh=mesh, in_specs=(placed, placed), out_specs=placed, check_vma=False)
```

time: 471 us -> 53.4 us (0.11)
  the two profiles are of different devices: /device:TPU:224 before, /device:TPU:1 now
where the time goes in v1:
time: 53.4 us; the launch traced here: 53.3 us
  Pallas kernels  50.8 us (95%)
  local copies, waits for them, and re-layouts  2.47 us (5%)
    pallas_call x1, Pallas kernels, per_device(): pl.pallas_call(functools.partial(kernel, nw, nn), out_shape=jax.ShapeDtyp...  50.8 us
    unnamed x5, local copies, waits for them, and re-layouts  2.47 us

profile of v1, /device:TPU:1, one launch (start us, length us, event | category | flops | bytes accessed | tf_op | source)
XLA Modules:
  0.0 53.3 jit_solution(1903443768295053534)
XLA Ops:
  0.0 0.0 copy-start
  0.0 0.9 %copy-done = f32[8,16,256]{2,1,0:T(8,128)S(1)} copy-done((f32[8,16,256]{2,1,0:T(8,128)S(1)}, f32[8,16,256]{2,1,0:T(8,128)}, u32[]{:S(2)}) %copy-start) | copy-done | bytes 131096
  0.9 0.0 copy-start.1
  0.9 0.9 %copy-done.1 = f32[8,16,256]{2,1,0:T(8,128)S(1)} copy-done((f32[8,16,256]{2,1,0:T(8,128)S(1)}, f32[8,16,256]{2,1,0:T(8,128)}, u32[]{:S(2)}) %copy-start.1) | copy-done | bytes 131096
  1.8 50.8 %shard_map.28 = f32[8,16,256]{2,1,0:T(8,128)S(1)} custom-call(f32[8,16,256]{2,1,0:T(8,128)S(1)} %copy-done, f32[8,16,256]{2,1,0:T(8,128)S(1)} %copy-done.1), custom_call_target="tpu_custom_call" | custom-call | tf_op jit(solution)/shard_map/pallas_call | solution.py:584
  52.6 0.7 %copy.4 = f32[8,16,256]{2,1,0:T(8,128)} copy(f32[8,16,256]{2,1,0:T(8,128)S(1)} %shard_map.28) | data formatting | bytes 262144
Async XLA Ops:
  0.0 0.9 %copy-start = (f32[8,16,256]{2,1,0:T(8,128)S(1)}, f32[8,16,256]{2,1,0:T(8,128)}, u32[]{:S(2)}) copy-start(f32[8,16,256]{2,1,0:T(8,128)} %r_in.1) | copy-start | bytes 393220
  0.9 0.9 %copy-start.1 = (f32[8,16,256]{2,1,0:T(8,128)S(1)}, f32[8,16,256]{2,1,0:T(8,128)}, u32[]{:S(2)}) copy-start(f32[8,16,256]{2,1,0:T(8,128)} %k_in.1) | copy-start | bytes 393220

commit v2 on v1

--- a/solution.py
+++ b/solution.py
@@ -15,6 +15,7 @@
 OWN = 7
 PLANES = 22
 HALO_K, HALO_R = 7, 6
+BY_WEIGHTS, BY_FIRST, BY_SWEEP, BY_RESIDUAL, BY_LAST = 4, 10, 3, 2, 4
 OWN1 = 3
 PLANES1 = 10
 
@@ -58,79 +59,107 @@
     return zero_one(fine // 2 == coarse)
 
 
-def weights(first, last, k, wx, wy, wz, diag, inv):
+def reciprocal(x):
+    guess = pl.reciprocal(x, approx=True)
+    return guess * (2.0 - x * guess)
+
+
+def weights(k, wx, wy, wz, diag, inv):
     rows, columns = k.shape[1:]
     lane = lax.broadcasted_iota(jnp.int32, (rows, columns), 1)
     rim = jnp.where((lane == 0) | (lane == columns - 1), 0.5, 0.0)
     half = jnp.where(lane == columns - 1, 0.0, 0.5)
-    wx[first - 1] = 0.5 * (k[first - 1] + k[first])
 
     def plane(p):
         here = k[p]
         x = 0.5 * (here + k[p + 1])
+        lower = 0.5 * (here + k[p - 1])
         y = 0.5 * (here + pltpu.roll(here, rows - 1, 0))
         z = half * (here + pltpu.roll(here, columns - 1, 1))
-        d = (x + wx[p - 1]) + (y + pltpu.roll(y, 1, 0)) + (z + pltpu.roll(z, 1, 1)) + rim * here
+        d = (x + lower) + (y + pltpu.roll(y, 1, 0)) + (z + pltpu.roll(z, 1, 1)) + rim * here
         wx[p] = x
         wy[p] = y
         wz[p] = z
         diag[p] = d
-        inv[p] = jnp.where(here > 0.0, OMEGA / d, 0.0)
+        inv[p] = jnp.where(here > 0.0, OMEGA * reciprocal(d), 0.0)
 
     return plane
 
 
-def image_at(p, v, wx, wy, wz, diag):
+def pull_at(p, v, wx, wy, wz, keep=None):
     rows, columns = v.shape[1:]
+    keep = rows if keep is None else keep
     here = v[p]
     y, z = wy[p], wz[p]
-    total = wx[p] * v[p + 1] + wx[p - 1] * v[p - 1]
-    total += y * pltpu.roll(here, rows - 1, 0) + pltpu.roll(y * here, 1, 0)
+    total = wx[p, :keep] * v[p + 1, :keep] + wx[p - 1, :keep] * v[p - 1, :keep]
+    total += y[:keep] * pltpu.roll(here, rows - 1, 0)[:keep] + pltpu.roll(y * here, 1, 0)[:keep]
+    here, z = here[:keep], z[:keep]
     total += z * pltpu.roll(here, columns - 1, 1) + pltpu.roll(z * here, 1, 1)
-    return diag[p] * here - total
-
-
-def loop(first, last, body, unroll):
-    if unroll:
+    return total
+
+
+def loop(first, last, body, by):
+    if last - first <= by:
         for p in range(first, last):
             body(p)
-    else:
-
-        def step(p, carry):
-            body(p)
-            return carry
-
-        lax.fori_loop(first, last, step, 0)
-
-
-def corner_pack(k, r, x_low, y_low):
+        return
+
+    def step(i, carry):
+        for p in range(by):
+            body(first + i * by + p)
+        return carry
+
+    whole = (last - first) // by
+    lax.fori_loop(0, whole, step, 0)
+    for p in range(first + whole * by, last):
+        body(p)
+
+
+def turns(y_low):
+    return lambda x, by: pltpu.roll(x, (by if y_low else -by) % 8, 0)
+
+
+def from_corner(y_low):
     sub = lax.broadcasted_iota(jnp.int32, (8, 256), 0)
-    near = 7 - sub if y_low else sub
-    turn = lambda x, by: pltpu.roll(x, (by if y_low else -by) % 8, 0)
+    return 7 - sub if y_low else sub
+
+
+def pack_k(k, y_low):
+    near, turn = from_corner(y_low), turns(y_low)
     return [
-        jnp.where(near < 6, k(1), turn(k(5), 2)),
-        jnp.where(near < 5, k(2), turn(r(3), 3)),
-        jnp.where(near < 4, k(3), turn(r(2), 4)),
-        jnp.where(near < 5, r(1), turn(k(4), 3)),
-        jnp.where(near < 2, r(4), jnp.where(near == 2, turn(r(5), -2), turn(k(6), -3))),
+        jnp.where(near < 6, k[0], turn(k[4], 2)),
+        jnp.where(near < 5, k[1], turn(k[3], 3)),
+        jnp.where(near < 4, k[2], turn(k[5], 4)),
     ]
 
 
-def corner_unpack(tiles, y_low):
-    turn = lambda x, by: pltpu.roll(x, (by if y_low else -by) % 8, 0)
-    one, two, three, four, five = tiles
-    k = [one, two, three, turn(four, -3), turn(one, -2), turn(five, 3)]
-    r = [four, turn(three, -4), turn(two, -3), five, turn(five, 2)]
-    return k, r
+def unpack_k(tiles, y_low):
+    turn = turns(y_low)
+    one, two, three = tiles
+    return [one, two, three, turn(two, -3), turn(one, -2), turn(three, -4)]
+
+
+def pack_r(r, y_low):
+    near, turn = from_corner(y_low), turns(y_low)
+    return [
+        jnp.where(near < 5, r[0], turn(r[2], 3)),
+        jnp.where(near < 4, r[1], jnp.where(near >= 6, turn(r[3], 2), turn(r[4], 4))),
+    ]
+
+
+def unpack_r(tiles, y_low):
+    turn = turns(y_low)
+    one, two = tiles
+    return [one, two, turn(one, -3), turn(two, -2), turn(two, -4)]
 
 
 def kernel(nw, nn, r_in, k_in, out, *refs):
-    (K0, R0, EA, EB, WX, WY, WZ, DG, IV, XS, CS, CR, T0,
+    (K0, R0, EA, EB, WX, WY, WZ, DG, IV, XS, CK, CKR, CR, CRR, T0, OUT,
      K1, R1, A1, B1, WX1, WY1, WZ1, DG1, IV1, E1S, E1G, T1,
      SB2, G2, KS, GK, K2X, K2S, K3S, K3G, R3S, R3G, F3,
      X3, Y3, Z3, D3, S3, Q3, P3, MB, E2G, E3, DS,
-     load, halo_s, halo_r, kz_s, kz_r, rz_s, rz_r, kx_s, kx_r, e1_s, e1_r,
-     k3_s, k3_r, r3_s, r3_r, e2_s, e2_r) = refs
+     load, halo_s, halo_r, tail_s, tail_r, kz_s, kz_r, rz_s, rz_r, kx_s, kx_r, e1_s, e1_r,
+     k3_s, k3_r, k4_s, k4_r, r3_s, r3_r, e2_s, e2_r) = refs
     w, n = lax.axis_index("wide"), lax.axis_index("narrow")
     wide = lambda d: lax.rem(w + (d + nw), nw)
     narrow = lambda d: lax.rem(n + (d + nn), nn)
@@ -189,9 +218,10 @@
         rows = pl.ds(8, 8) if dy > 0 else pl.ds(0, 8)
         at = lambda a: OWN + (8 - a if dx > 0 else a - 1)
         keep = jnp.where(outside(dx, dy) == 0, 1.0, 0.0).astype(F32)
-        tiles = corner_pack(lambda a: K0[at(a), rows], lambda a: R0[at(a), rows], dx > 0, dy > 0)
-        for t, tile in enumerate(tiles):
-            CS[i, t] = tile * keep
+        for t, tile in enumerate(pack_k([K0[at(a), rows] for a in range(1, 7)], dy > 0)):
+            CK[i, t] = tile * keep
+        for t, tile in enumerate(pack_r([R0[at(a), rows] for a in range(1, 6)], dy > 0)):
+            CR[i, t] = tile * keep
 
     fine, coarse = iotas(512, 128)
     to_quarter = zero_one(((fine // 256) == (coarse // 64)) & ((fine % 256) // 4 == coarse % 64))
@@ -207,29 +237,37 @@
 
     pl.semaphore_wait(barrier, (nw - 1) + 3 * (nn - 1))
 
-    halo = []
-
-    def push(src, dst, to):
-        i = len(halo)
-        halo.append(remote(src, dst, halo_s.at[i], halo_r.at[i], to))
-        halo[-1].start()
-
-    for dx in (-1, 1):
-        over = outside(dx, 0)
-        for ref, width in ((K0, HALO_K), (R0, HALO_R)):
-            start = OWN + 8 - width if dx > 0 else OWN
-            land = OWN - width if dx > 0 else OWN + 8
-            start = jnp.where(over == 1, PLANES, start)
-            push(ref.at[pl.ds(start, width), 0:16], ref.at[land : land + width, 0:16], (wide(dx), n))
-    for dy in (-1, 1):
-        over = outside(0, dy)
-        for ref in (K0, R0):
-            start = jnp.where(over == 1, PLANES, OWN)
+    def send_halo(ref, width, packed, landing, send, recv):
+        copies = []
+
+        def push(src, dst, to):
+            i = len(copies)
+            copies.append(remote(src, dst, send.at[i], recv.at[i], to))
+            copies[-1].start()
+
+        for dy in (-1, 1):
+            start = jnp.where(outside(0, dy) == 1, PLANES, OWN)
             rows = slice(8, 16) if dy > 0 else slice(0, 8)
             land = slice(24, 32) if dy > 0 else slice(16, 24)
             push(ref.at[pl.ds(start, 8), rows], ref.at[OWN : OWN + 8, land], (w, narrow(dy)))
-    for i, (dx, dy) in enumerate(corners):
-        push(CS.at[i], CR.at[3 - i], (wide(dx), narrow(dy)))
+        for dx in (-1, 1):
+            start = OWN + 8 - width if dx > 0 else OWN
+            land = OWN - width if dx > 0 else OWN + 8
+            start = jnp.where(outside(dx, 0) == 1, PLANES, start)
+            push(ref.at[pl.ds(start, width), 0:16], ref.at[land : land + width, 0:16], (wide(dx), n))
+        for i, (dx, dy) in enumerate(corners):
+            push(packed.at[i], landing.at[3 - i], (wide(dx), narrow(dy)))
+        return copies
+
+    def place_corners(ref, landing, unpack, count):
+        for i, (dx, dy) in enumerate(corners):
+            tiles = unpack([landing[i, t] for t in range(count)], dy < 0)
+            rows = pl.ds(24, 8) if dy < 0 else pl.ds(16, 8)
+            for a, tile in enumerate(tiles, 1):
+                ref[OWN - a if dx < 0 else OWN + 7 + a, rows] = tile
+
+    halo = send_halo(K0, HALO_K, CK, CKR, halo_s, halo_r)
+    tail = send_halo(R0, HALO_R, CR, CRR, tail_s, tail_r)
 
     def gather_k(d, carry):
         remote(KS, GK.at[n], kz_s.at[0], kz_r.at[0], (w, narrow(d))).start()
@@ -240,37 +278,69 @@
 
     for copy in halo:
         copy.wait_recv()
-    for i, (dx, dy) in enumerate(corners):
-        k, r = corner_unpack([CR[i, t] for t in range(5)], dy < 0)
-        rows = pl.ds(24, 8) if dy < 0 else pl.ds(16, 8)
-        at = lambda a: OWN - a if dx < 0 else OWN + 7 + a
-        for a in range(1, 7):
-            K0[at(a), rows] = k[a - 1]
-        for a in range(1, 6):
-            R0[at(a), rows] = r[a - 1]
-
-    level0 = (WX, WY, WZ, DG)
-    set_weights = weights(1, 21, K0, WX, WY, WZ, DG, IV)
+    place_corners(K0, CKR, unpack_k, 3)
+    WX[0] = 0.5 * (K0[0] + K0[1])
+    loop(1, 21, weights(K0, WX, WY, WZ, DG, IV), BY_WEIGHTS)
+
+    remote(GK.at[0 : nn - 1], GK.at[0 : nn - 1], kz_s.at[0], kz_r.at[0], (w, n)).wait_recv()
+    for i in range(nn):
+        K2X[0, 4 * i : 4 * i + 4] = GK[i]
+    slab_k = K2X[0]
+    beside = (-2, -1, 1, 2)
+    kx = []
+    for i, dx in enumerate(beside):
+        copy = remote(K2X.at[outside(dx, 0)], K2S.at[2 - dx], kx_s.at[i], kx_r.at[i], (wide(dx), n))
+        copy.start()
+        kx.append(copy)
+    K2S[2] = slab_k
+
+    row, lane = iotas(32, 128)
+    own_chunk = (row // 8) == (lane // 32)
+    fine, coarse = iotas(128, 128)
+    fold = zero_one((fine % 64) // 2 == coarse % 32)
+    unfold = zero_one((coarse % 64) // 2 == fine % 32)
+
+    def to_level3(x):
+        spread = jnp.where(own_chunk, times_right(x, fold), 0.0)
+        T1[...] = (spread[0:8] + spread[8:16]) + (spread[16:24] + spread[24:32])
+        return T1[pl.ds(0, 4, stride=2)] + T1[pl.ds(1, 4, stride=2)]
+
+    ny = nw // 8
+    in_row, in_column = lax.rem(w, 8), w // 8
+    K3S[...] = 0.125 * to_level3(slab_k)
+
+    def along_y(d, carry):
+        remote(K3S, K3G.at[in_row, in_column], k3_s.at[0], k3_r.at[0], (wide(8 * d), n)).start()
+        return carry
+
+    lax.fori_loop(1, ny, along_y, 0)
+    K3G[in_row, in_column] = K3S[...]
+
+    for copy in tail:
+        copy.wait_recv()
+    place_corners(R0, CRR, unpack_r, 2)
+
+    level0 = (WX, WY, WZ)
 
     def first0(p):
-        set_weights(p)
         EA[p] = IV[p] * R0[p]
 
-    loop(1, 21, first0, False)
+    loop(1, 21, first0, BY_FIRST)
 
     def sweep0(source, target):
         def plane(p):
-            target[p] = source[p] + IV[p] * (R0[p] - image_at(p, source, *level0))
+            target[p] = (1.0 - OMEGA) * source[p] + IV[p] * (R0[p] + pull_at(p, source, *level0))
 
         return plane
 
-    loop(2, 20, sweep0(EA, EB), False)
+    loop(2, 20, sweep0(EA, EB), BY_SWEEP)
 
     def residual0(i):
         p = 2 * i + 3
-        XS[i] = (R0[p] - image_at(p, EB, *level0)) + (R0[p + 1] - image_at(p + 1, EB, *level0))
-
-    loop(0, 8, residual0, False)
+        one, two = ((R0[q] - DG[q] * EB[q]) + pull_at(q, EB, *level0) for q in (p, p + 1))
+        XS[i] = one + two
+
+    loop(0, 8, residual0, BY_RESIDUAL)
     halve = halve_z()
     T0[0:256] = times_right(XS[...].reshape(256, 256), halve)
     R1[1:9] = (0.5 * (T0[pl.ds(0, 128, stride=2)] + T0[pl.ds(1, 128, stride=2)])).reshape(8, 16, 128)
@@ -278,22 +348,21 @@
     T0[...] = times_right(k_pairs, halve)
     K1[...] = (0.125 * (T0[pl.ds(0, 160, stride=2)] + T0[pl.ds(1, 160, stride=2)])).reshape(PLANES1, 16, 128)
 
-    level1 = (WX1, WY1, WZ1, DG1)
-    set_weights1 = weights(1, 9, K1, WX1, WY1, WZ1, DG1, IV1)
-
-    def first1(q):
+    level1 = (WX1, WY1, WZ1)
+    set_weights1 = weights(K1, WX1, WY1, WZ1, DG1, IV1)
+
+    def sweep1(source, target):
+        def plane(q):
+            target[q] = (1.0 - OMEGA) * source[q] + IV1[q] * (R1[q] + pull_at(q, source, *level1))
+
+        return plane
+
+    WX1[0] = 0.5 * (K1[0] + K1[1])
+    for q in range(1, 9):
         set_weights1(q)
         A1[q] = IV1[q] * R1[q]
-
-    def sweep1(source, target):
-        def plane(q):
-            target[q] = source[q] + IV1[q] * (R1[q] - image_at(q, source, *level1))
-
-        return plane
-
-    loop(1, 9, first1, True)
-    loop(2, 8, sweep1(A1, B1), True)
-    left = [R1[q] - image_at(q, B1, *level1) for q in range(OWN1, OWN1 + 4)]
+    loop(2, 8, sweep1(A1, B1), 8)
+    left = [(R1[q] - DG1[q] * B1[q]) + pull_at(q, B1, *level1) for q in range(OWN1, OWN1 + 4)]
     fine, coarse = iotas(256, 128)
     halve_pair = zero_one(((fine // 128) == (coarse // 64)) & ((fine % 128) // 2 == coarse % 64))
     pair = jnp.concatenate([(left[0] + left[1])[0:8], (left[2] + left[3])[0:8]], axis=1)
@@ -327,28 +396,15 @@
         copy.start()
         near.append(copy)
 
-    remote(GK.at[0 : nn - 1], GK.at[0 : nn - 1], kz_s.at[0], kz_r.at[0], (w, n)).wait_recv()
-    for i in range(nn):
-        K2X[0, 4 * i : 4 * i + 4] = GK[i]
-    slab_k = K2X[0]
-    beside = (-2, -1, 1, 2)
-    kx = []
-    for i, dx in enumerate(beside):
-        copy = remote(K2X.at[outside(dx, 0)], K2S.at[2 - dx], kx_s.at[i], kx_r.at[i], (wide(dx), n))
-        copy.start()
-        kx.append(copy)
-    K2S[2] = slab_k
-
-    row, lane = iotas(32, 128)
-    own_chunk = (row // 8) == (lane // 32)
-    fine, coarse = iotas(128, 128)
-    fold = zero_one((fine % 64) // 2 == coarse % 32)
-    unfold = zero_one((coarse % 64) // 2 == fine % 32)
-
-    def to_level3(x):
-        spread = jnp.where(own_chunk, times_right(x, fold), 0.0)
-        T1[...] = (spread[0:8] + spread[8:16]) + (spread[16:24] + spread[24:32])
-        return T1[pl.ds(0, 4, stride=2)] + T1[pl.ds(1, 4, stride=2)]
+    column = K3G.at[0, 0 : ny - 1]
+    remote(column, column, k3_s.at[0], k3_r.at[0], (w, n)).wait_recv()
+
+    def along_row(d, carry):
+        to = 8 * in_column + lax.rem(in_row + d, 8)
+        remote(K3G.at[in_row], K3G.at[in_row], k4_s.at[0], k4_r.at[0], (to, n)).start()
+        return carry
+
+    lax.fori_loop(1, 8, along_row, 0)
 
     def to_all(src, dst, send, recv):
         def one(d, carry):
@@ -360,9 +416,6 @@
 
     def from_all(dst, send, recv):
         return remote(dst.at[0 : nw - 1], dst.at[0 : nw - 1], send.at[0], recv.at[0], (w, n))
-
-    K3S[...] = 0.125 * to_level3(slab_k)
-    to_all(K3S, K3G, k3_s, k3_r)
 
     for copy in kx:
         copy.wait_recv()
@@ -431,17 +484,18 @@
         K1[OWN1 + x1, 8:16] = rim1(x1, 2)
         if -2 <= x1 <= 5:
             R1[OWN1 + x1, 8:16] = rim1(x1, 1)
-    loop(1, 9, set_weights1, True)
-
-    from_all(K3G, k3_s, k3_r).wait_recv()
+    WX1[0] = 0.5 * (K1[0] + K1[1])
+    loop(1, 9, set_weights1, 8)
+
+    remote(K3G.at[0:7], K3G.at[0:7], k4_s.at[0], k4_r.at[0], (w, n)).wait_recv()
 
     def in_order(gathered, target):
         for i in range(nw):
-            F3[4 * i : 4 * i + 4] = gathered[i]
+            F3[4 * i : 4 * i + 4] = gathered(i)
         for j in range(4):
             target[j] = F3[pl.ds(j, nw, stride=4)]
 
-    in_order(K3G, P3)
+    in_order(lambda i: K3G[i % 8, i // 8], P3)
     row, lane = iotas(nw, 128)
     last_chunk, first_chunk = lane >= 96, lane < 32
     for j in range(4):
@@ -465,7 +519,7 @@
         D3[j] = d + rim * here
 
     from_all(R3G, r3_s, r3_r).wait_recv()
-    in_order(R3G, Q3)
+    in_order(lambda i: R3G[i], Q3)
     norm = jnp.zeros((nw, 128), F32)
     for j in range(4):
         P3[j] = Q3[j]
@@ -535,8 +589,8 @@
                     rim = rim1(x1, 0)
                     A1[OWN1 + x1, 0:8] = mine + grown[0:8, 128 * p : 128 * p + 128]
                     A1[OWN1 + x1, 8:16] = rim + grown[8:16, 128 * p : 128 * p + 128]
-    loop(1, 9, sweep1(A1, B1), True)
-    loop(2, 8, sweep1(B1, A1), True)
+    loop(1, 9, sweep1(A1, B1), 8)
+    loop(2, 8, sweep1(B1, A1), 8)
 
     stretched = times_right(A1[2:8].reshape(96, 128), double_z())
     i, j = iotas(32, 16)
@@ -545,20 +599,25 @@
         grown = times_left(twice, stretched[16 * q : 16 * q + 16])
         for p in (5 + 2 * q, 6 + 2 * q):
             EA[p] = EB[p] + grown
-    loop(6, 16, sweep0(EA, EB), False)
+    loop(6, 16, sweep0(EA, EB), BY_SWEEP)
 
     def last(p):
-        value = EB[p] + IV[p] * (R0[p] - image_at(p, EB, *level0))
-        out[p - OWN] = value[0:16]
-
-    loop(7, 15, last, False)
-
-    for copy in halo + near + kx + e2x:
+        here = EB[p, 0:16]
+        out[p - OWN] = (1.0 - OMEGA) * here + IV[p, 0:16] * (R0[p, 0:16] + pull_at(p, EB, *level0, keep=16))
+
+    done = []
+    for i, first in enumerate((OWN, OWN + 4)):
+        loop(first, first + 4, last, BY_LAST)
+
+    for copy in halo + tail + near + kx + e2x:
         copy.wait_send()
     remote(GK.at[0 : nn - 1], GK.at[0 : nn - 1], kz_s.at[0], kz_r.at[0], (w, n)).wait_send()
     remote(arrived, arrived, rz_s.at[0], rz_r.at[0], (w, n)).wait_send()
-    from_all(K3G, k3_s, k3_r).wait_send()
+    remote(column, column, k3_s.at[0], k3_r.at[0], (w, n)).wait_send()
+    remote(K3G.at[0:7], K3G.at[0:7], k4_s.at[0], k4_r.at[0], (w, n)).wait_send()
     from_all(R3G, r3_s, r3_r).wait_send()
+    for copy in done:
+        copy.wait()
 
 
 def solution(mesh):
@@ -572,23 +631,24 @@
         vmem = lambda *shape: pltpu.VMEM(shape, F32)
         dma = lambda count: pltpu.SemaphoreType.DMA((count,))
         scratch = [with_zeros, with_zeros] + [fine] * 7
-        scratch += [vmem(8, 32, 256), vmem(4, 5, 8, 256), vmem(4, 5, 8, 256), vmem(320, 128)]
+        scratch += [vmem(8, 32, 256), vmem(4, 3, 8, 256), vmem(4, 3, 8, 256), vmem(4, 2, 8, 256), vmem(4, 2, 8, 256)]
+        scratch += [vmem(320, 128), vmem(8, 16, 256)]
         scratch += [middle] * 9 + [vmem(2, 4, 3, 8, 128), vmem(8, 4, 3, 8, 128), vmem(8, 128)]
         scratch += [vmem(2, 4, 128), vmem(3 * nn, 4, 128), vmem(4, 128), vmem(nn, 4, 128)]
         scratch += [vmem(2, 32, 128), vmem(5, 32, 128)]
-        scratch += [vmem(4, 128), vmem(nw, 4, 128), vmem(4, 128), vmem(nw, 4, 128), vmem(4 * nw, 128)]
+        scratch += [vmem(4, 128), vmem(8, nw // 8, 4, 128), vmem(4, 128), vmem(nw, 4, 128), vmem(4 * nw, 128)]
         scratch += [coarse] * 7
         scratch += [vmem(2, 2, 32, 128), vmem(5, 2, 32, 128), vmem(4, nw + 16, 128), vmem(40, 128)]
-        scratch += [dma(2), dma(12), dma(12), dma(1), dma(1), dma(1), dma(1), dma(4), dma(4), dma(8), dma(8)]
-        scratch += [dma(1), dma(1), dma(1), dma(1), dma(4), dma(4)]
+        scratch += [dma(2), dma(8), dma(8), dma(8), dma(8), dma(1), dma(1), dma(1), dma(1), dma(4), dma(4), dma(8), dma(8)]
+        scratch += [dma(1), dma(1), dma(1), dma(1), dma(1), dma(1), dma(4), dma(4)]
         return pl.pallas_call(
             functools.partial(kernel, nw, nn),
             out_shape=jax.ShapeDtypeStruct((8, 16, 256), F32),
-            in_specs=[pl.BlockSpec(memory_space=pl.ANY)] * 2,
+            in_specs=[pl.BlockSpec(memory_space=pltpu.HBM)] * 2,
             out_specs=pl.BlockSpec(memory_space=pltpu.VMEM),
             scratch_shapes=scratch,
             compiler_params=pltpu.CompilerParams(
-                collective_id=0, has_side_effects=True, vmem_limit_bytes=40 * 1024 * 1024
+                collective_id=0, has_side_effects=True, vmem_limit_bytes=55040 * 1024
             ),
         )(right_side, coefficient)
 

time: 53.4 us -> 45.4 us (0.85)
  Pallas kernels: 50.8 us -> 44.7 us
  local copies, waits for them, and re-layouts: 2.47 us -> 0.66 us
    pallas_call x1, Pallas kernels: 50.8 us -> 44.7 us  [per_device(): pl.pallas_call(functools.partial(kernel, nw, nn), out_shape=jax.ShapeDtyp...]
    unnamed x5 -> x1, local copies, waits for them, and re-layouts: 2.47 us -> 0.66 us
where the time goes in v2:
time: 45.4 us; the launch traced here: 45.3 us
  Pallas kernels  44.7 us (98%)
  local copies, waits for them, and re-layouts  0.66 us (1%)
    pallas_call x1, Pallas kernels, per_device(): pl.pallas_call(functools.partial(kernel, nw, nn), out_shape=jax.ShapeDtyp...  44.7 us

profile of v2, /device:TPU:1, one launch (start us, length us, event | category | flops | bytes accessed | tf_op | source)
XLA Modules:
  0.0 45.3 jit_solution(12128669544878904794)
XLA Ops:
  0.0 44.7 %shard_map.28 = f32[8,16,256]{2,1,0:T(8,128)S(1)} custom-call(f32[8,16,256]{2,1,0:T(8,128)} %r_in.1, f32[8,16,256]{2,1,0:T(8,128)} %k_in.1), custom_call_target="tpu_custom_call" | custom-call | tf_op jit(solution)/shard_map/pallas_call | solution.py:644
  44.7 0.7 %copy.4 = f32[8,16,256]{2,1,0:T(8,128)} copy(f32[8,16,256]{2,1,0:T(8,128)S(1)} %shard_map.28) | data formatting | bytes 262144

commit v3 on v2

--- a/solution.py
+++ b/solution.py
@@ -98,6 +98,10 @@
     return total
 
 
+def far_first(size):
+    return sorted(range(1, size), key=lambda d: -min(d, size - d))
+
+
 def loop(first, last, body, by):
     if last - first <= by:
         for p in range(first, last):
@@ -164,6 +168,9 @@
     wide = lambda d: lax.rem(w + (d + nw), nw)
     narrow = lambda d: lax.rem(n + (d + nn), nn)
 
+    ny = nw // 8
+    in_row, in_column = lax.rem(w, 8), w // 8
+
     def outside(dx, dy):
         over = jnp.int32(0)
         if dx:
@@ -185,17 +192,23 @@
     load_r.start()
     barrier = pltpu.get_barrier_semaphore()
 
-    def greet_wide(d, carry):
-        pl.semaphore_signal(barrier, inc=1, device_id=(wide(d), n), device_id_type=MESH)
-        return carry
-
-    def greet_narrow(d, carry):
-        for dx in (-1, 0, 1):
-            pl.semaphore_signal(barrier, inc=1, device_id=(wide(dx), narrow(d)), device_id_type=MESH)
-        return carry
-
-    lax.fori_loop(1, nn, greet_narrow, 0)
-    lax.fori_loop(1, nw, greet_wide, 0)
+    def greet(to):
+        pl.semaphore_signal(barrier, inc=1, device_id=to, device_id_type=MESH)
+
+    for dx in (-1, 1):
+        for dy in (-1, 1):
+            greet((wide(dx), narrow(dy)))
+    ring_z, ring_y = far_first(nn), far_first(ny)
+    for d in ring_z:
+        greet((w, narrow(d)))
+    for dx in (-1, 1):
+        greet((wide(dx), n))
+        greet((wide(2 * dx), n))
+    for d in ring_y:
+        greet((wide(8 * d), n))
+    for d in range(1, 8):
+        greet((8 * in_column + lax.rem(in_row + d, 8), n))
+    greeted = 4 + len(ring_z) + 4 + len(ring_y) + 7
 
     zero_planes = jnp.zeros((8, 16, 256), F32)
     K0[PLANES : PLANES + 8, 0:16] = zero_planes
@@ -235,7 +248,7 @@
     )
     KS[...] = quarter * (1.0 / 64.0)
 
-    pl.semaphore_wait(barrier, (nw - 1) + 3 * (nn - 1))
+    pl.semaphore_wait(barrier, greeted)
 
     def send_halo(ref, width, packed, landing, send, recv):
         copies = []
@@ -266,21 +279,12 @@
             for a, tile in enumerate(tiles, 1):
                 ref[OWN - a if dx < 0 else OWN + 7 + a, rows] = tile
 
+    for d in far_first(nn):
+        remote(KS, GK.at[n], kz_s.at[0], kz_r.at[0], (w, narrow(d))).start()
+    GK[n] = KS[...]
+
     halo = send_halo(K0, HALO_K, CK, CKR, halo_s, halo_r)
     tail = send_halo(R0, HALO_R, CR, CRR, tail_s, tail_r)
-
-    def gather_k(d, carry):
-        remote(KS, GK.at[n], kz_s.at[0], kz_r.at[0], (w, narrow(d))).start()
-        return carry
-
-    lax.fori_loop(1, nn, gather_k, 0)
-    GK[n] = KS[...]
-
-    for copy in halo:
-        copy.wait_recv()
-    place_corners(K0, CKR, unpack_k, 3)
-    WX[0] = 0.5 * (K0[0] + K0[1])
-    loop(1, 21, weights(K0, WX, WY, WZ, DG, IV), BY_WEIGHTS)
 
     remote(GK.at[0 : nn - 1], GK.at[0 : nn - 1], kz_s.at[0], kz_r.at[0], (w, n)).wait_recv()
     for i in range(nn):
@@ -305,16 +309,17 @@
         T1[...] = (spread[0:8] + spread[8:16]) + (spread[16:24] + spread[24:32])
         return T1[pl.ds(0, 4, stride=2)] + T1[pl.ds(1, 4, stride=2)]
 
-    ny = nw // 8
-    in_row, in_column = lax.rem(w, 8), w // 8
     K3S[...] = 0.125 * to_level3(slab_k)
 
-    def along_y(d, carry):
+    for d in far_first(ny):
         remote(K3S, K3G.at[in_row, in_column], k3_s.at[0], k3_r.at[0], (wide(8 * d), n)).start()
-        return carry
-
-    lax.fori_loop(1, ny, along_y, 0)
     K3G[in_row, in_column] = K3S[...]
+
+    for copy in halo:
+        copy.wait_recv()
+    place_corners(K0, CKR, unpack_k, 3)
+    WX[0] = 0.5 * (K0[0] + K0[1])
+    loop(1, 21, weights(K0, WX, WY, WZ, DG, IV), BY_WEIGHTS)
 
     for copy in tail:
         copy.wait_recv()
@@ -341,6 +346,16 @@
         XS[i] = one + two
 
     loop(0, 8, residual0, BY_RESIDUAL)
+    column = K3G.at[0, 0 : ny - 1]
+    remote(column, column, k3_s.at[0], k3_r.at[0], (w, n)).wait_recv()
+
+    def along_row(d, carry):
+        to = 8 * in_column + lax.rem(in_row + d, 8)
+        remote(K3G.at[in_row], K3G.at[in_row], k4_s.at[0], k4_r.at[0], (to, n)).start()
+        return carry
+
+    lax.fori_loop(1, 8, along_row, 0)
+
     halve = halve_z()
     T0[0:256] = times_right(XS[...].reshape(256, 256), halve)
     R1[1:9] = (0.5 * (T0[pl.ds(0, 128, stride=2)] + T0[pl.ds(1, 128, stride=2)])).reshape(8, 16, 128)
@@ -370,15 +385,12 @@
     T0[0:16] = times_right(pair, halve_pair)
     SB2[0] = 0.5 * (T0[pl.ds(0, 4, stride=2)] + T0[pl.ds(1, 4, stride=2)])
 
-    def gather_r(d, carry):
-        for dx in (-1, 0, 1):
+    for copy in kx:
+        copy.wait_recv()
+    for d in far_first(nn) + [0]:
+        for dx in (-1, 1, 0) if d else (-1, 1):
             src = SB2.at[outside(dx, 0)]
             remote(src, G2.at[(1 - dx) * nn + n], rz_s.at[0], rz_r.at[0], (wide(dx), narrow(d))).start()
-        return carry
-
-    lax.fori_loop(1, nn, gather_r, 0)
-    for dx in (-1, 1):
-        remote(SB2.at[outside(dx, 0)], G2.at[(1 - dx) * nn + n], rz_s.at[0], rz_r.at[0], (wide(dx), n)).start()
     G2[nn + n] = SB2[0]
 
     for x1 in range(4):
@@ -396,29 +408,23 @@
         copy.start()
         near.append(copy)
 
-    column = K3G.at[0, 0 : ny - 1]
-    remote(column, column, k3_s.at[0], k3_r.at[0], (w, n)).wait_recv()
-
-    def along_row(d, carry):
-        to = 8 * in_column + lax.rem(in_row + d, 8)
-        remote(K3G.at[in_row], K3G.at[in_row], k4_s.at[0], k4_r.at[0], (to, n)).start()
-        return carry
-
-    lax.fori_loop(1, 8, along_row, 0)
-
     def to_all(src, dst, send, recv):
-        def one(d, carry):
-            remote(src, dst.at[w], send.at[0], recv.at[0], (wide(d), n)).start()
-            return carry
-
-        lax.fori_loop(1, nw, one, 0)
+        def one(to):
+            remote(src, dst.at[w], send.at[0], recv.at[0], (to, n)).start()
+
+        def column_of(y, d):
+            return 8 * lax.rem(in_column + y, ny) + lax.rem(in_row + d, 8)
+
+        for y in far_first(ny):
+            for d in (4, 5, 3, 2, 6, 7, 1, 0):
+                one(column_of(y, d))
+        for d in (4, 5, 3, 2, 6, 7, 1):
+            one(column_of(0, d))
         dst[w] = src[...]
 
     def from_all(dst, send, recv):
         return remote(dst.at[0 : nw - 1], dst.at[0 : nw - 1], send.at[0], recv.at[0], (w, n))
 
-    for copy in kx:
-        copy.wait_recv()
     k2 = K2S[...]
     row = lax.broadcasted_iota(jnp.int32, (5, 32, 128), 1)
     cell = lax.broadcasted_iota(jnp.int32, (5, 32, 128), 2)
@@ -460,6 +466,7 @@
     e2 = e2 + inv2[some] * (r2 - image2(e2, some))
     left2 = (r2 - image2(e2, some))[1]
     R3S[...] = 0.5 * to_level3(left2)
+    remote(K3G.at[0:7], K3G.at[0:7], k4_s.at[0], k4_r.at[0], (w, n)).wait_recv()
     to_all(R3S, R3G, r3_s, r3_r)
 
     MB[0, 0] = e2[1]
@@ -487,7 +494,6 @@
     WX1[0] = 0.5 * (K1[0] + K1[1])
     loop(1, 9, set_weights1, 8)
 
-    remote(K3G.at[0:7], K3G.at[0:7], k4_s.at[0], k4_r.at[0], (w, n)).wait_recv()
 
     def in_order(gathered, target):
         for i in range(nw):
@@ -523,11 +529,10 @@
     norm = jnp.zeros((nw, 128), F32)
     for j in range(4):
         P3[j] = Q3[j]
-        S3[j] = jnp.zeros((nw, 128), F32)
         norm += Q3[j] * Q3[j]
     norm = jnp.sum(norm, keepdims=True)
 
-    def iteration(step, norm):
+    for step in range(COARSE_ITERS):
         images = []
         dot = jnp.zeros((nw, 128), F32)
         carried = pltpu.roll(Y3[3] * P3[3], 32, 1)
@@ -542,19 +547,21 @@
             images.append(image)
             dot += v * image
         alpha = norm / jnp.sum(dot, keepdims=True)
+        if step == COARSE_ITERS - 1:
+            for j in range(4):
+                S3[j] = S3[j] + alpha * P3[j]
+            break
         following = jnp.zeros((nw, 128), F32)
         for j in range(4):
-            S3[j] = S3[j] + alpha * P3[j]
             rest = Q3[j] - alpha * images[j]
             Q3[j] = rest
             following += rest * rest
         following = jnp.sum(following, keepdims=True)
         beta = following / norm
         for j in range(4):
+            S3[j] = (S3[j] + alpha * P3[j]) if step else alpha * P3[j]
             P3[j] = Q3[j] + beta * P3[j]
-        return following
-
-    lax.fori_loop(0, COARSE_ITERS, iteration, norm)
+        norm = following
     for j in range(4):
         E3[j, 8 : 8 + nw] = S3[j]
 
@@ -652,5 +659,5 @@
             ),
         )(right_side, coefficient)
 
-    placed = P("wide", "narrow", None)
+    placed = P("wide", "narrow")
     return jax.shard_map(per_device, mesh=mesh, in_specs=(placed, placed), out_specs=placed, check_vma=False)

time: 45.4 us -> 43.1 us (0.949)
  Pallas kernels: 44.7 us -> 42.3 us
    pallas_call x1, Pallas kernels: 44.7 us -> 42.3 us  [per_device(): pl.pallas_call(functools.partial(kernel, nw, nn), out_shape=jax.ShapeDtyp...]
where the time goes in v3:
time: 43.1 us; the launch traced here: 42.9 us
  Pallas kernels  42.3 us (98%)
  local copies, waits for them, and re-layouts  0.66 us (2%)
    pallas_call x1, Pallas kernels, per_device(): pl.pallas_call(functools.partial(kernel, nw, nn), out_shape=jax.ShapeDtyp...  42.3 us

profile of v3, /device:TPU:1, one launch (start us, length us, event | category | flops | bytes accessed | tf_op | source)
XLA Modules:
  0.0 42.9 jit_solution(14823822809314688735)
XLA Ops:
  0.0 42.3 %shard_map.28 = f32[8,16,256]{2,1,0:T(8,128)S(1)} custom-call(f32[8,16,256]{2,1,0:T(8,128)} %r_in.1, f32[8,16,256]{2,1,0:T(8,128)} %k_in.1), custom_call_target="tpu_custom_call" | custom-call | tf_op jit(solution)/shard_map/pallas_call | solution.py:651
  42.3 0.7 %copy.4 = f32[8,16,256]{2,1,0:T(8,128)} copy(f32[8,16,256]{2,1,0:T(8,128)S(1)} %shard_map.28) | data formatting | bytes 262144

commit v4 on v3

--- a/solution.py
+++ b/solution.py
@@ -15,7 +15,7 @@
 OWN = 7
 PLANES = 22
 HALO_K, HALO_R = 7, 6
-BY_WEIGHTS, BY_FIRST, BY_SWEEP, BY_RESIDUAL, BY_LAST = 4, 10, 3, 2, 4
+BY_WEIGHTS, BY_FIRST, BY_SWEEP, BY_RESIDUAL, BY_LAST = 5, 20, 9, 8, 4
 OWN1 = 3
 PLANES1 = 10
 
@@ -161,7 +161,7 @@
     (K0, R0, EA, EB, WX, WY, WZ, DG, IV, XS, CK, CKR, CR, CRR, T0, OUT,
      K1, R1, A1, B1, WX1, WY1, WZ1, DG1, IV1, E1S, E1G, T1,
      SB2, G2, KS, GK, K2X, K2S, K3S, K3G, R3S, R3G, F3,
-     X3, Y3, Z3, D3, S3, Q3, P3, MB, E2G, E3, DS,
+     X3, Y3, Z3, D3, S3, Q3, P3, A3, MB, E2G, E3, DS,
      load, halo_s, halo_r, tail_s, tail_r, kz_s, kz_r, rz_s, rz_r, kx_s, kx_r, e1_s, e1_r,
      k3_s, k3_r, k4_s, k4_r, r3_s, r3_r, e2_s, e2_r) = refs
     w, n = lax.axis_index("wide"), lax.axis_index("narrow")
@@ -222,7 +222,7 @@
     K2X[1] = jnp.zeros((32, 128), F32)
     MB[1] = jnp.zeros((2, 32, 128), F32)
     E1S[1] = jnp.zeros((4, 3, 8, 128), F32)
-    E3[...] = jnp.zeros((4, nw + 16, 128), F32)
+    E3[...] = jnp.zeros((4, 8, 16, 128), F32)
     load_k.wait()
     load_r.wait()
 
@@ -321,6 +321,15 @@
     WX[0] = 0.5 * (K0[0] + K0[1])
     loop(1, 21, weights(K0, WX, WY, WZ, DG, IV), BY_WEIGHTS)
 
+    halve = halve_z()
+    k_pairs = jnp.concatenate([K0[2 * q + 1] + K0[2 * q + 2] for q in range(PLANES1)], axis=0)
+    T0[...] = times_right(k_pairs, halve)
+    K1[...] = (0.125 * (T0[pl.ds(0, 160, stride=2)] + T0[pl.ds(1, 160, stride=2)])).reshape(PLANES1, 16, 128)
+    level1 = (WX1, WY1, WZ1)
+    set_weights1 = weights(K1, WX1, WY1, WZ1, DG1, IV1)
+    WX1[0] = 0.5 * (K1[0] + K1[1])
+    loop(1, 9, set_weights1, 8)
+
     for copy in tail:
         copy.wait_recv()
     place_corners(R0, CRR, unpack_r, 2)
@@ -356,25 +365,15 @@
 
     lax.fori_loop(1, 8, along_row, 0)
 
-    halve = halve_z()
     T0[0:256] = times_right(XS[...].reshape(256, 256), halve)
     R1[1:9] = (0.5 * (T0[pl.ds(0, 128, stride=2)] + T0[pl.ds(1, 128, stride=2)])).reshape(8, 16, 128)
-    k_pairs = jnp.concatenate([K0[2 * q + 1] + K0[2 * q + 2] for q in range(PLANES1)], axis=0)
-    T0[...] = times_right(k_pairs, halve)
-    K1[...] = (0.125 * (T0[pl.ds(0, 160, stride=2)] + T0[pl.ds(1, 160, stride=2)])).reshape(PLANES1, 16, 128)
-
-    level1 = (WX1, WY1, WZ1)
-    set_weights1 = weights(K1, WX1, WY1, WZ1, DG1, IV1)
-
     def sweep1(source, target):
         def plane(q):
             target[q] = (1.0 - OMEGA) * source[q] + IV1[q] * (R1[q] + pull_at(q, source, *level1))
 
         return plane
 
-    WX1[0] = 0.5 * (K1[0] + K1[1])
     for q in range(1, 9):
-        set_weights1(q)
         A1[q] = IV1[q] * R1[q]
     loop(2, 8, sweep1(A1, B1), 8)
     left = [(R1[q] - DG1[q] * B1[q]) + pull_at(q, B1, *level1) for q in range(OWN1, OWN1 + 4)]
@@ -494,29 +493,37 @@
     WX1[0] = 0.5 * (K1[0] + K1[1])
     loop(1, 9, set_weights1, 8)
 
-
     def in_order(gathered, target):
         for i in range(nw):
             F3[4 * i : 4 * i + 4] = gathered(i)
         for j in range(4):
-            target[j] = F3[pl.ds(j, nw, stride=4)]
+            for t in range(8):
+                target[j, t] = F3[pl.ds(4 * t + j, 8, stride=32)]
+
+    def next_x(v):
+        return jnp.concatenate([v[1:], pltpu.roll(v[0], 7, 0)[None]], axis=0)
+
+    def last_x(v):
+        return jnp.concatenate([pltpu.roll(v[7], 1, 0)[None], v[:7]], axis=0)
 
     in_order(lambda i: K3G[i % 8, i // 8], P3)
-    row, lane = iotas(nw, 128)
+    cube = (8, 8, 128)
+    tile, row, lane = (lax.broadcasted_iota(jnp.int32, cube, d) for d in range(3))
+    first_x, final_x = (tile == 0) & (row == 0), (tile == 7) & (row == 7)
     last_chunk, first_chunk = lane >= 96, lane < 32
     for j in range(4):
         here = P3[j]
-        X3[j] = jnp.where(row == nw - 1, 0.0, 0.5 * (here + pltpu.roll(here, nw - 1, 0)))
-        Z3[j] = jnp.where(lane % 32 == 31, 0.0, 0.5 * (here + pltpu.roll(here, 127, 1)))
+        X3[j] = jnp.where(final_x, 0.0, 0.5 * (here + next_x(here)))
+        Z3[j] = jnp.where(lane % 32 == 31, 0.0, 0.5 * (here + pltpu.roll(here, 127, 2)))
         if j < 3:
             Y3[j] = 0.5 * (here + P3[j + 1])
         else:
-            Y3[j] = jnp.where(last_chunk, 0.0, 0.5 * (here + pltpu.roll(P3[0], 96, 1)))
+            Y3[j] = jnp.where(last_chunk, 0.0, 0.5 * (here + pltpu.roll(P3[0], 96, 2)))
     for j in range(4):
         here = P3[j]
-        lower = Y3[j - 1] if j else pltpu.roll(Y3[3], 32, 1)
-        d = (X3[j] + pltpu.roll(X3[j], 1, 0)) + (Y3[j] + lower) + (Z3[j] + pltpu.roll(Z3[j], 1, 1))
-        rim = jnp.where((row == 0) | (row == nw - 1), 0.5, 0.0)
+        lower = Y3[j - 1] if j else pltpu.roll(Y3[3], 32, 2)
+        d = (X3[j] + last_x(X3[j])) + (Y3[j] + lower) + (Z3[j] + pltpu.roll(Z3[j], 1, 2))
+        rim = jnp.where(first_x | final_x, 0.5, 0.0)
         rim += jnp.where((lane % 32 == 0) | (lane % 32 == 31), 0.5, 0.0)
         if j == 0:
             rim += jnp.where(first_chunk, 0.5, 0.0)
@@ -526,48 +533,52 @@
 
     from_all(R3G, r3_s, r3_r).wait_recv()
     in_order(lambda i: R3G[i], Q3)
-    norm = jnp.zeros((nw, 128), F32)
-    for j in range(4):
-        P3[j] = Q3[j]
-        norm += Q3[j] * Q3[j]
-    norm = jnp.sum(norm, keepdims=True)
-
+
+    def total_of(v):
+        return jnp.sum(v.reshape(64, 128), keepdims=True).reshape(1, 1, 1)
+
+    def image3(v):
+        images = []
+        carried = pltpu.roll(Y3[3] * v[3], 32, 2)
+        for j in range(4):
+            x, y, z = X3[j], Y3[j], Z3[j]
+            total = x * next_x(v[j]) + last_x(x * v[j])
+            total += z * pltpu.roll(v[j], 127, 2) + pltpu.roll(z * v[j], 1, 2)
+            total += y * (v[j + 1] if j < 3 else pltpu.roll(v[0], 96, 2)) + carried
+            carried = y * v[j]
+            images.append(D3[j] * v[j] - total)
+        return images
+
+    norm = alpha = None
     for step in range(COARSE_ITERS):
-        images = []
-        dot = jnp.zeros((nw, 128), F32)
-        carried = pltpu.roll(Y3[3] * P3[3], 32, 1)
+        images = image3(Q3)
+        one, two = jnp.zeros(cube, F32), jnp.zeros(cube, F32)
         for j in range(4):
-            v = P3[j]
-            x, y, z = X3[j], Y3[j], Z3[j]
-            total = x * pltpu.roll(v, nw - 1, 0) + pltpu.roll(x * v, 1, 0)
-            total += z * pltpu.roll(v, 127, 1) + pltpu.roll(z * v, 1, 1)
-            total += y * (P3[j + 1] if j < 3 else pltpu.roll(P3[0], 96, 1)) + carried
-            carried = y * v
-            image = D3[j] * v - total
-            images.append(image)
-            dot += v * image
-        alpha = norm / jnp.sum(dot, keepdims=True)
-        if step == COARSE_ITERS - 1:
-            for j in range(4):
-                S3[j] = S3[j] + alpha * P3[j]
-            break
-        following = jnp.zeros((nw, 128), F32)
+            rest = Q3[j]
+            one += rest * rest
+            two += rest * images[j]
+        following, pull = total_of(one), total_of(two)
+        if step:
+            beta = following / norm
+            alpha = following / (pull - beta * (following / alpha))
+        else:
+            alpha = following / pull
+        norm = following
         for j in range(4):
-            rest = Q3[j] - alpha * images[j]
-            Q3[j] = rest
-            following += rest * rest
-        following = jnp.sum(following, keepdims=True)
-        beta = following / norm
+            direction = Q3[j] + beta * P3[j] if step else Q3[j]
+            result = S3[j] + alpha * direction if step else alpha * direction
+            if step == COARSE_ITERS - 1:
+                E3[j, :, 1:9] = result
+                continue
+            carried = images[j] + beta * A3[j] if step else images[j]
+            P3[j], A3[j], S3[j] = direction, carried, result
+            Q3[j] = Q3[j] - alpha * carried
+
+    for i in range(5):
+        x = w + (6 + i)
         for j in range(4):
-            S3[j] = (S3[j] + alpha * P3[j]) if step else alpha * P3[j]
-            P3[j] = Q3[j] + beta * P3[j]
-        norm = following
-    for j in range(4):
-        E3[j, 8 : 8 + nw] = S3[j]
-
-    for i in range(5):
-        for j in range(4):
-            DS[8 * i + 2 * j : 8 * i + 2 * j + 2] = jnp.broadcast_to(E3[j, pl.ds(w + (6 + i), 1)], (2, 128))
+            value = E3[j, lax.rem(x, 8), pl.ds(x // 8, 1)]
+            DS[8 * i + 2 * j : 8 * i + 2 * j + 2] = jnp.broadcast_to(value, (2, 128))
     chunk = lax.broadcasted_iota(jnp.int32, (8, 128), 1) // 32
     rows = [jnp.where(chunk == c, DS[8 * i : 8 * i + 8], 0.0) for i in range(5) for c in range(4)]
     added = times_right(jnp.concatenate(rows, axis=0), unfold).reshape(5, 32, 128)
@@ -634,7 +645,7 @@
         fine = pltpu.VMEM((PLANES, 32, 256), F32)
         with_zeros = pltpu.VMEM((PLANES + 8, 32, 256), F32)
         middle = pltpu.VMEM((PLANES1, 16, 128), F32)
-        coarse = pltpu.VMEM((4, nw, 128), F32)
+        coarse = pltpu.VMEM((4, 8, 8, 128), F32)
         vmem = lambda *shape: pltpu.VMEM(shape, F32)
         dma = lambda count: pltpu.SemaphoreType.DMA((count,))
         scratch = [with_zeros, with_zeros] + [fine] * 7
@@ -644,8 +655,8 @@
         scratch += [vmem(2, 4, 128), vmem(3 * nn, 4, 128), vmem(4, 128), vmem(nn, 4, 128)]
         scratch += [vmem(2, 32, 128), vmem(5, 32, 128)]
         scratch += [vmem(4, 128), vmem(8, nw // 8, 4, 128), vmem(4, 128), vmem(nw, 4, 128), vmem(4 * nw, 128)]
-        scratch += [coarse] * 7
-        scratch += [vmem(2, 2, 32, 128), vmem(5, 2, 32, 128), vmem(4, nw + 16, 128), vmem(40, 128)]
+        scratch += [coarse] * 8
+        scratch += [vmem(2, 2, 32, 128), vmem(5, 2, 32, 128), vmem(4, 8, 16, 128), vmem(40, 128)]
         scratch += [dma(2), dma(8), dma(8), dma(8), dma(8), dma(1), dma(1), dma(1), dma(1), dma(4), dma(4), dma(8), dma(8)]
         scratch += [dma(1), dma(1), dma(1), dma(1), dma(1), dma(1), dma(4), dma(4)]
         return pl.pallas_call(

time: 43.1 us -> 41.9 us (0.972)
  Pallas kernels: 42.3 us -> 41.1 us
    pallas_call x1, Pallas kernels: 42.3 us -> 41.1 us  [per_device(): pl.pallas_call(functools.partial(kernel, nw, nn), out_shape=jax.ShapeDtyp...]
where the time goes in v4:
time: 41.9 us; the launch traced here: 41.7 us
  Pallas kernels  41.1 us (98%)
  local copies, waits for them, and re-layouts  0.66 us (2%)
    pallas_call x1, Pallas kernels, per_device(): pl.pallas_call(functools.partial(kernel, nw, nn), out_shape=jax.ShapeDtyp...  41.1 us

profile of v4, /device:TPU:1, one launch (start us, length us, event | category | flops | bytes accessed | tf_op | source)
XLA Modules:
  0.0 41.7 jit_solution(7625963365263426413)
XLA Ops:
  0.0 41.1 %shard_map.28 = f32[8,16,256]{2,1,0:T(8,128)S(1)} custom-call(f32[8,16,256]{2,1,0:T(8,128)} %r_in.1, f32[8,16,256]{2,1,0:T(8,128)} %k_in.1), custom_call_target="tpu_custom_call" | custom-call | tf_op jit(solution)/shard_map/pallas_call | solution.py:662
  41.1 0.7 %copy.4 = f32[8,16,256]{2,1,0:T(8,128)} copy(f32[8,16,256]{2,1,0:T(8,128)S(1)} %shard_map.28) | data formatting | bytes 262144

commit v5 on v4

--- a/solution.py
+++ b/solution.py
@@ -163,7 +163,7 @@
      SB2, G2, KS, GK, K2X, K2S, K3S, K3G, R3S, R3G, F3,
      X3, Y3, Z3, D3, S3, Q3, P3, A3, MB, E2G, E3, DS,
      load, halo_s, halo_r, tail_s, tail_r, kz_s, kz_r, rz_s, rz_r, kx_s, kx_r, e1_s, e1_r,
-     k3_s, k3_r, k4_s, k4_r, r3_s, r3_r, e2_s, e2_r) = refs
+     k3_s, k3_r, k4_s, k4_r, r3_s, r3_r, e2_s, e2_r, k5_s, k5_r) = refs
     w, n = lax.axis_index("wide"), lax.axis_index("narrow")
     wide = lambda d: lax.rem(w + (d + nw), nw)
     narrow = lambda d: lax.rem(n + (d + nn), nn)
@@ -330,6 +330,17 @@
     WX1[0] = 0.5 * (K1[0] + K1[1])
     loop(1, 9, set_weights1, 8)
 
+    for x1 in range(4):
+        E1S[0, x1, 2] = K1[OWN1 + x1, 0:8]
+    around = [(dx, dy) for dx in (-1, 0, 1) for dy in (-1, 0, 1) if dx or dy]
+    ahead = []
+    for i, (dx, dy) in enumerate(corners):
+        at = around.index((dx, dy))
+        planes = slice(1, 4) if dx > 0 else slice(0, 3)
+        src, dst = E1S.at[outside(dx, dy)].at[planes, 2:3], E1G.at[7 - at].at[planes, 2:3]
+        ahead.append(remote(src, dst, k5_s.at[i], k5_r.at[i], (wide(dx), narrow(dy))))
+        ahead[-1].start()
+
     for copy in tail:
         copy.wait_recv()
     place_corners(R0, CRR, unpack_r, 2)
@@ -395,13 +406,11 @@
     for x1 in range(4):
         E1S[0, x1, 0] = B1[OWN1 + x1, 0:8]
         E1S[0, x1, 1] = R1[OWN1 + x1, 0:8]
-        E1S[0, x1, 2] = K1[OWN1 + x1, 0:8]
-    around = [(dx, dy) for dx in (-1, 0, 1) for dy in (-1, 0, 1) if dx or dy]
     near = []
     for i, (dx, dy) in enumerate(around):
         src, dst = E1S.at[outside(dx, dy)], E1G.at[7 - i]
         planes = slice(1, 4) if dx > 0 else (slice(0, 3) if dx < 0 else slice(0, 4))
-        arrays = slice(0, 3) if dx and dy else slice(0, 1)
+        arrays = slice(0, 2) if dx and dy else slice(0, 1)
         src, dst = src.at[planes, arrays], dst.at[planes, arrays]
         copy = remote(src, dst, e1_s.at[i], e1_r.at[i], (wide(dx), narrow(dy)))
         copy.start()
@@ -477,7 +486,7 @@
         e2x.append(copy)
     E2G[2] = MB[0]
 
-    for copy in near:
+    for copy in ahead + near:
         copy.wait_recv()
     sub = lax.broadcasted_iota(jnp.int32, (8, 128), 0)
 
@@ -627,7 +636,7 @@
     for i, first in enumerate((OWN, OWN + 4)):
         loop(first, first + 4, last, BY_LAST)
 
-    for copy in halo + tail + near + kx + e2x:
+    for copy in halo + tail + ahead + near + kx + e2x:
         copy.wait_send()
     remote(GK.at[0 : nn - 1], GK.at[0 : nn - 1], kz_s.at[0], kz_r.at[0], (w, n)).wait_send()
     remote(arrived, arrived, rz_s.at[0], rz_r.at[0], (w, n)).wait_send()
@@ -658,7 +667,7 @@
         scratch += [coarse] * 8
         scratch += [vmem(2, 2, 32, 128), vmem(5, 2, 32, 128), vmem(4, 8, 16, 128), vmem(40, 128)]
         scratch += [dma(2), dma(8), dma(8), dma(8), dma(8), dma(1), dma(1), dma(1), dma(1), dma(4), dma(4), dma(8), dma(8)]
-        scratch += [dma(1), dma(1), dma(1), dma(1), dma(1), dma(1), dma(4), dma(4)]
+        scratch += [dma(1), dma(1), dma(1), dma(1), dma(1), dma(1), dma(4), dma(4), dma(4), dma(4)]
         return pl.pallas_call(
             functools.partial(kernel, nw, nn),
             out_shape=jax.ShapeDtypeStruct((8, 16, 256), F32),

time: 41.9 us -> 41.9 us (level)
  no operation moved by 1% of the time
where the time goes in v5:
time: 41.9 us; the launch traced here: 41.8 us
  Pallas kernels  41.1 us (98%)
  local copies, waits for them, and re-layouts  0.66 us (2%)
    pallas_call x1, Pallas kernels, per_device(): pl.pallas_call(functools.partial(kernel, nw, nn), out_shape=jax.ShapeDtyp...  41.1 us

profile of v5, /device:TPU:1, one launch (start us, length us, event | category | flops | bytes accessed | tf_op | source)
XLA Modules:
  0.0 41.8 jit_solution(11282428579710596810)
XLA Ops:
  0.0 41.1 %shard_map.28 = f32[8,16,256]{2,1,0:T(8,128)S(1)} custom-call(f32[8,16,256]{2,1,0:T(8,128)} %r_in.1, f32[8,16,256]{2,1,0:T(8,128)} %k_in.1), custom_call_target="tpu_custom_call" | custom-call | tf_op jit(solution)/shard_map/pallas_call | solution.py:671
  41.1 0.7 %copy.4 = f32[8,16,256]{2,1,0:T(8,128)} copy(f32[8,16,256]{2,1,0:T(8,128)S(1)} %shard_map.28) | data formatting | bytes 262144
